TPU v7x, 768 devices: a whole 4x8x12 slice. The times are simulated.
768 devices in a mesh: row: 64 (over x, y, core), col: 12 (over z).
Axes of the slice: x: 4, y: 8, z: 12, core: 2. Of those that a mesh axis runs over, the one named last changes fastest.
Arguments:
- momentum: float32 [16384, 13824], P('row', 'col'), may hold values from -0.6 to 0.6
- gradient: bfloat16 [16384, 13824], P('row', 'col'), may hold values from -36 to 36
- right_factor: float32 [13824, 256], P('col'), may hold values from -0.0546875 to 0.0546875
Outputs:
- new_momentum: float32 [16384, 13824], P('row', 'col')
- new_right: float32 [13824, 256], P('col')
- update: bfloat16 [16384, 13824], P('row', 'col')
All inputs are finite; a program needn't handle non-finite values.
Results may differ from a plain program's by a relative error of at most 0.001.
Values sent between devices are 32-bit elements; how exact they have to be, the bound alone decides.
No kernel may reach another device: no remote copies, remote signals or barrier semaphores. Data moves between devices by JAX's collectives and lax.ppermute only.
A program may use at most 32 MiB of HBM per device.

v0:
```python
import math

import jax
import jax.numpy as jnp
from jax import lax
from jax.sharding import PartitionSpec as P

ROWS = 16384
COLS = 13824
RANK = 256


decay_rate = 0.95
epsilon = 1e-06


def on_device(momentum, gradient, right_factor):
    highest = lax.Precision.HIGHEST
    blended = momentum + gradient.astype(jnp.float32)
    left_local = jnp.dot(
        blended, right_factor, precision=highest, preferred_element_type=jnp.float32
    )
    left_raw = lax.psum(left_local, "col")
    gram_local = jnp.dot(
        left_raw.T, left_raw, precision=highest, preferred_element_type=jnp.float32
    )
    gram_matrix = lax.psum(gram_local, "row")
    lower_factor = jnp.linalg.cholesky(gram_matrix)
    orthonormal = jax.scipy.linalg.solve_triangular(lower_factor, left_raw.T, lower=True).T
    right_local = jnp.dot(
        blended.T, orthonormal, precision=highest, preferred_element_type=jnp.float32
    )
    right_full = lax.psum(right_local, "row")
    squares = lax.psum(jnp.sum(right_full * right_full, axis=0), "col")
    new_momentum = blended - (1.0 - decay_rate) * jnp.dot(
        orthonormal, right_full.T, precision=highest, preferred_element_type=jnp.float32
    )
    new_right = right_full / jnp.sqrt(squares + epsilon)
    factor = math.sqrt(ROWS * COLS / RANK)
    update = (
        factor
        * jnp.dot(orthonormal, new_right.T, precision=highest, preferred_element_type=jnp.float32)
    ).astype(jnp.bfloat16)
    return (new_momentum, new_right, update)


def solution(mesh):
    return jax.shard_map(
        on_device,
        mesh=mesh,
        in_specs=(P("row", "col"), P("row", "col"), P("col", None)),
        out_specs=(P("row", "col"), P("col", None), P("row", "col")),
        check_vma=False,
    )
```

profile of v0, /device:TPU:1, one launch (start us, length us, event | category | flops | bytes accessed | tf_op | source)
XLA Modules:
  0.0 641.9 jit_solution(10682343223683953351)
XLA Ops:
  7.2 0.0 copy-start
  7.2 0.0 all-reduce.5.cloned.1.call-start
  7.2 1.2 copy-done
  8.4 3.4 fusion.3
  11.8 0.0 all-reduce.5.cloned.1.call-update
  11.9 0.0 all-reduce.7.cloned.1.call-start
  11.9 112.2 %all-reduce.5.cloned.1.call-done = f32[256,256]{1,0:T(8,128)} async-done(((f32[256,256]{1,0:T(8,128)}), f32[256,256]{1,0:T(8,128)}) %all-reduce.5.cloned.1.call-update) | async-done | bytes 262160 | tf_op jit(solution)/shard_map/psum | solution.py:23
  124.1 2.3 fusion.16
  126.5 0.0 all-reduce.7.cloned.1.call-update
  126.5 0.0 all-reduce.9.cloned.1.call-start
  126.6 203.7 %all-reduce.7.cloned.1.call-done = f32[256,256]{0,1:T(8,128)} async-done(((f32[256,256]{0,1:T(8,128)}), f32[256,256]{0,1:T(8,128)}) %all-reduce.7.cloned.1.call-update) | async-done | bytes 262160 | tf_op jit(solution)/shard_map/psum | solution.py:27
  330.3 1.1 copy.7
  331.3 1.0 fusion.4
  332.3 11.7 %cholesky.50 = f32[128,128]{1,0:T(8,128)S(1)} custom-call(f32[128,128]{1,0:T(8,128)S(1)} %cholesky.118), custom_call_target="Cholesky" | custom-call | tf_op jit(solution)/shard_map/jit(cholesky)/cholesky | solution.py:28
  344.1 9.8 %custom-call.15 = f32[1,128,128]{1,2,0:T(8,128)S(1)} custom-call(f32[1,128,128]{2,1,0:T(8,128)S(1)} %get-tuple-element.24), custom_call_target="InvertDiagBlocksLowerTriangular" | custom-call | tf_op jit(solution)/shard_map/jit(cholesky)/cholesky | solution.py:28
  353.9 0.0 copy-start.8
  354.0 0.2 constant_dynamic-update-slice_fusion.1
  354.2 0.3 convolution_subtract_fusion.1
  354.4 11.7 %cholesky.105 = f32[128,128]{1,0:T(8,128)S(1)} custom-call(f32[128,128]{1,0:T(8,128)S(1)} %convolution_subtract_fusion.1), custom_call_target="Cholesky" | custom-call | tf_op jit(solution)/shard_map/jit(cholesky)/cholesky | solution.py:28
  366.2 0.7 compare_reduce_fusion
  368.0 0.0 copy-start.1
  368.1 0.0 copy-start.3
  368.1 1.1 select_select_fusion
  369.2 0.1 triangular_solve.57
  369.3 5.3 while.1
  369.4 0.6 fusion.27
  370.0 2.0 bitcast_dynamic-update-slice_fusion.2
  372.0 0.6 fusion.27
  372.6 2.0 bitcast_dynamic-update-slice_fusion.2
  374.6 21.1 %custom-call.16 = f32[2,128,128]{1,2,0:T(8,128)} custom-call(f32[2,128,128]{2,1,0:T(8,128)} %get-tuple-element.10), custom_call_target="InvertDiagBlocksLowerTriangular" | custom-call | tf_op jit(solution)/shard_map/jit(_solve_triangular)/triangular_solve | solution.py:29
  395.7 1.1 fusion.5
  396.9 0.0 copy-start.6
  396.9 0.4 convolution_subtract_fusion
  397.3 1.2 fusion.8
  398.4 0.0 copy-start.9
  398.5 0.6 copy-done.9
  399.1 0.0 copy-done.3
  399.1 3.0 fusion.2
  402.1 0.0 all-reduce.9.cloned.1.call-update
  402.2 204.5 %all-reduce.9.cloned.1.call-done = f32[1152,256]{1,0:T(8,128)} async-done(((f32[1152,256]{1,0:T(8,128)}), f32[1152,256]{1,0:T(8,128)}) %all-reduce.9.cloned.1.call-update) | async-done | bytes 1179664 | tf_op jit(solution)/shard_map/psum | solution.py:33
  606.7 1.5 multiply_reduce_fusion
  608.2 19.8 %psum.31 = f32[256]{0:T(256)S(1)} all-reduce(f32[256]{0:T(256)S(1)} %multiply_reduce_fusion), channel_id=1, replica_groups=mesh['row'=64,'col'=12] {'col'}, use_global_device_ids=true, to_apply=%region_8.9 | all-reduce | flops 256 | bytes 2048 | tf_op jit(solution)/shard_map/psum | solution.py:34
  628.1 0.0 copy-start.10
  628.1 0.1 broadcast_divide_fusion
  628.2 0.8 copy-done.7
  629.0 0.1 copy-done.10
  629.1 3.0 fusion.1
  632.1 3.2 fusion
  (21 shorter events, 0.1 us)
Async XLA Ops:
  7.2 1.3 copy-start
  7.2 117.0 %all-reduce.5.cloned.1.call-start = ((), (), s32[]{:S(2)}) async-start(), calls=%async_computation | async-start | bytes 524288 | tf_op jit(solution)/shard_map/psum | solution.py:23
  11.9 318.4 %all-reduce.7.cloned.1.call-start = ((), (), s32[]{:S(2)}) async-start(), calls=%async_computation.1 | async-start | bytes 524288 | tf_op jit(solution)/shard_map/psum | solution.py:27
  126.5 480.2 %all-reduce.9.cloned.1.call-start = ((), (), s32[]{:S(2)}) async-start(), calls=%async_computation.2 | async-start | bytes 2359296 | tf_op jit(solution)/shard_map/psum | solution.py:33
  353.9 41.8 %copy-start.8 = (f32[256,256]{1,0:T(8,128)S(1)}, f32[256,256]{1,0:T(8,128)}, u32[]{:S(2)}) copy-start(f32[256,256]{1,0:T(8,128)} %all-reduce.5.cloned.1.call-done) | copy-start | bytes 786436
  366.2 1.9 copy-start.11
  368.0 31.1 %copy-start.1 = (f32[256,1152]{1,0:T(8,128)S(1)}, f32[256,1152]{1,0:T(8,128)}, u32[]{:S(2)}) copy-start(f32[256,1152]{1,0:T(8,128)} %param.3) | copy-start | bytes 3538948
  368.1 31.0 %copy-start.3 = (bf16[256,1152]{1,0:T(8,128)(2,1)S(1)}, bf16[256,1152]{1,0:T(8,128)(2,1)}, u32[]{:S(2)}) copy-start(bf16[256,1152]{1,0:T(8,128)(2,1)} %param.4) | copy-start | bytes 1769476
  396.9 1.6 copy-start.6
  398.4 0.7 copy-start.9
  606.7 21.4 %copy-start.2 = (f32[1152,256]{1,0:T(8,128)S(1)}, f32[1152,256]{1,0:T(8,128)}, u32[]{:S(2)}) copy-start(f32[1152,256]{1,0:T(8,128)} %all-reduce.9.cloned.1.call-done) | copy-start | bytes 3538948
  628.1 0.9 copy-start.7
  628.1 1.0 copy-start.10
  629.1 6.3 copy-start.5
  629.1 3.0 copy-start.4
Sparse Core Ops, SparseCore 0:
  12.0 112.1 all-reduce.4
  128.6 201.6 all-reduce.6
  402.3 204.3 all-reduce.8
where the time goes:
time: 648 us; the launch traced here: 642 us
  waiting for transfers between devices  521 us (80%)
  other arithmetic  58.8 us (9%)
  blocking collectives  19.8 us (3%)
  matrix products  18.2 us (3%)
  between operations  15.1 us (2%)
  local copies, waits for them, and re-layouts  9.14 us (1%)
    psum x1, waiting for transfers between devices, on_device(): right_full = lax.psum(right_local, 'row')  205 us
    psum x1, waiting for transfers between devices, on_device(): gram_matrix = lax.psum(gram_local, 'row')  204 us
    psum x1, waiting for transfers between devices, on_device(): left_raw = lax.psum(left_local, 'col')  112 us
    another operation x6, other arithmetic, on_device(): lower_factor = jnp.linalg.cholesky(gram_matrix)  34 us
    another operation x3, other arithmetic, on_device(): jax.scipy.linalg.solve_triangular(lower_factor, left_raw.T, lower=True)  22.2 us
    psum x1, blocking collectives, on_device(): squares = lax.psum(jnp.sum(right_full * right_full, axis=0), 'col')  19.8 us
  transfers between devices with their start and end apart: 3, of which 3 were waited for; matrix products, arithmetic and copies ran while one was open for 0% of the time, Pallas kernels for 0%

commit v1 on v0

v1 whole, which is shorter than its diff:
```python
import math

import jax
import jax.numpy as jnp
from jax import lax
from jax.experimental import pallas as pl
from jax.experimental.pallas import tpu as pltpu
from jax.sharding import Mesh
from jax.sharding import PartitionSpec as P

ROWS = 16384
COLS = 13824
RANK = 256
BLOCK = 32

decay_rate = 0.95
epsilon = 1e-06

ROW = ("x", "y", "core")
SWAP = ((0, 1), (1, 0))
HIGHEST = lax.Precision.HIGHEST


def dot(a, b, contract):
    return lax.dot_general(
        a, b, ((contract[0], contract[1]), ((), ())), precision=HIGHEST, preferred_element_type=jnp.float32
    )


def exchange(parts, axes):
    return lax.all_to_all(parts, axes, 0, 0, tiled=True)


def scatter_sum(parts, axes):
    return jnp.sum(exchange(parts, axes), axis=0)


def gather(part, axes, count):
    return exchange(jnp.broadcast_to(part, (count,) + part.shape), axes)


def wide(a):
    return jnp.concatenate([a, a], axis=1)


def invert_panel(panel, low):
    pieces = len(panel)
    row8 = lax.broadcasted_iota(jnp.int32, (8, 128), 0)
    lane = lax.broadcasted_iota(jnp.int32, (8, 128), 1)
    unit = [(row8 + 8 * r == lane).astype(jnp.float32) for r in range(pieces)]
    scales = []
    for g in range(pieces):
        columns = []
        for i in range(8):
            at = low + 8 * g + i
            columns.append([
                jnp.broadcast_to(panel[r][:, at : at + 1], (8, 128)) if r >= g else None for r in range(pieces)
            ])
        pivots = jnp.zeros((8, 128), jnp.float32)
        factors = []
        for i in range(8):
            pivot = columns[i][g][i : i + 1, :]
            pivots = jnp.where(row8 == i, pivot, pivots)
            inverse = 1.0 / pivot
            factor = [columns[i][r] * inverse if r >= g else None for r in range(pieces)]
            factor[g] = jnp.where(row8 > i, factor[g], 0.0)
            factors.append(factor)
            for l in range(i + 1, 8):
                head = columns[l][g][i : i + 1, :]
                for r in range(g, pieces):
                    columns[l][r] = columns[l][r] - factor[r] * head
        for i in range(8):
            panel_row = panel[g][i : i + 1, :]
            unit_row = unit[g][i : i + 1, :]
            for r in range(g, pieces):
                panel[r] = panel[r] - wide(factors[i][r]) * panel_row
                unit[r] = unit[r] - factors[i][r] * unit_row
        scales.append(lax.rsqrt(pivots))
    panel = [panel[r] * wide(scales[r]) for r in range(pieces)]
    unit = [unit[r] * scales[r] for r in range(pieces)]
    return panel, unit


def split3(a):
    high = a.astype(jnp.bfloat16)
    rest = a - high.astype(jnp.float32)
    middle = rest.astype(jnp.bfloat16)
    return high, middle, (rest - middle.astype(jnp.float32)).astype(jnp.bfloat16)


def invert_factor_kernel(gram_ref, out_ref):
    out_ref[...] = gram_ref[...]
    for low in range(0, RANK, BLOCK):
        high = low + BLOCK
        panel = [out_ref[low + r : low + r + 8, :] for r in range(0, BLOCK, 8)]
        panel, unit = invert_panel(panel, low)
        out_ref[low:high, :] = jnp.concatenate(panel, axis=0)
        out_ref[low:high, low:high] = jnp.concatenate(unit, axis=0)[:, :BLOCK]
        if high < RANK:
            left = RANK - high
            a, b, c = split3(out_ref[low:high, :])
            first = jnp.concatenate([a, a, b, a, b, c], axis=0)
            second = jnp.concatenate([a, b, a, c, b, a], axis=0)
            if high % 128 == 0:
                first = first[:, high:]
            change = lax.dot_general(
                first, second, (((0,), (0,)), ((), ())), preferred_element_type=jnp.float32
            )
            change = change[change.shape[0] - left :]
            lane = lax.broadcasted_iota(jnp.int32, (left, RANK), 1)
            old = jnp.where((lane >= low) & (lane < high), 0.0, out_ref[high:, :])
            out_ref[high:, :] = old - change
    row = lax.broadcasted_iota(jnp.int32, (RANK, RANK), 0)
    lane = lax.broadcasted_iota(jnp.int32, (RANK, RANK), 1)
    out_ref[...] = jnp.where(row >= lane, out_ref[...], 0.0)


def invert_factor(gram):
    return pl.pallas_call(
        invert_factor_kernel,
        out_shape=jax.ShapeDtypeStruct((RANK, RANK), jnp.float32),
        compiler_params=pltpu.CompilerParams(vmem_limit_bytes=8 << 20),
        cost_estimate=pl.CostEstimate(flops=10_000_000_000, bytes_accessed=524288, transcendentals=0),
        name="invert_factor",
    )(gram)


def on_device(momentum, gradient, right_factor):
    core = lax.axis_index("core")
    blended = momentum + gradient.astype(jnp.float32)
    left_local = dot(blended, right_factor, ((1,), (0,)))
    left_parts = jnp.pad(left_local, ((0, 32), (0, 0))).reshape(12, 24, RANK)
    left_raw = gather(scatter_sum(left_parts, "col"), "col", 12).reshape(288, RANK)[:256]

    gram_local = dot(left_raw, left_raw, ((0,), (0,))).reshape(2, 128, RANK)
    right_local = dot(blended, left_raw, ((0,), (0,))).reshape(2, 576, RANK)
    both = jnp.concatenate([right_local, gram_local], axis=1)
    mine = lax.dynamic_index_in_dim(both, core, 0, False)
    theirs = lax.ppermute(lax.dynamic_index_in_dim(both, 1 - core, 0, False), "core", SWAP)
    part = scatter_sum((mine + theirs).reshape(4, 176, RANK), "x")
    part = scatter_sum(jnp.pad(part, ((0, 16), (0, 0))).reshape(8, 24, RANK), "y")
    part = gather(part, "y", 8).reshape(192, RANK)[:176]
    part = gather(part, "x", 4).reshape(704, RANK)

    gram_mine = part[576:]
    gram_theirs = lax.ppermute(gram_mine, "core", SWAP)
    right_mine = part[:576]
    right_theirs = lax.ppermute(right_mine, "core", SWAP)

    def in_order(own, other):
        return jnp.concatenate([jnp.where(core == 0, own, other), jnp.where(core == 0, other, own)], axis=0)

    inverse = invert_factor(in_order(gram_mine, gram_theirs))
    right_raw = in_order(right_mine, right_theirs)
    orthonormal = dot(left_raw, inverse, ((1,), (1,)))
    right_full = dot(right_raw, inverse, ((1,), (1,)))
    squares = jnp.sum(right_full * right_full, axis=0, keepdims=True)
    squares = jnp.sum(gather(squares, "col", 12), axis=(0, 1))

    new_momentum = blended - (1.0 - decay_rate) * dot(orthonormal, right_full, ((1,), (1,)))
    new_right = right_full / jnp.sqrt(squares + epsilon)
    factor = math.sqrt(ROWS * COLS / RANK)
    update = (factor * dot(orthonormal, new_right, ((1,), (1,)))).astype(jnp.bfloat16)
    return (new_momentum, new_right, update)


def solution(mesh):
    fine = Mesh(mesh.devices.reshape(4, 8, 2, 12), ("x", "y", "core", "col"))
    return jax.shard_map(
        on_device,
        mesh=fine,
        in_specs=(P(ROW, "col"), P(ROW, "col"), P("col", None)),
        out_specs=(P(ROW, "col"), P("col", None), P(ROW, "col")),
        check_vma=False,
    )
```

time: 648 us -> 158 us (0.24)
  waiting for transfers between devices: 521 us -> 21.9 us
  blocking collectives: 19.8 us -> 82.4 us
  other arithmetic: 58.8 us -> 2.46 us
  starting transfers between devices: 0.12 us -> 23.3 us
  between operations: 15.1 us -> 0.87 us
  Pallas kernels: 0 us -> 7.97 us
    psum x3 -> x0, waiting for transfers between devices: 520 us -> none  [the longest x1 205 us: on_device(): right_full = lax.psum(right_local, 'row')]
    all_to_all x0 -> x5, blocking collectives: none -> 82.4 us  [exchange(): return lax.all_to_all(parts, axes, 0, 0, tiled=True)]
    another operation x9 -> x0, other arithmetic: 56.2 us -> none  [the longest x6 34 us: on_device(): lower_factor = jnp.linalg.cholesky(gram_matrix)]
    psum x1 -> x0, blocking collectives: 19.8 us -> none  [on_device(): squares = lax.psum(jnp.sum(right_full * right_full, axis=0), 'col')]
    all_to_all x0 -> x2, waiting for transfers between devices: none -> 19.8 us  [exchange(): return lax.all_to_all(parts, axes, 0, 0, tiled=True)]
    ppermute x0 -> x3, starting transfers between devices: none -> 14.6 us  [the longest x1 7.09 us: on_device(): gram_theirs = lax.ppermute(gram_mine, 'core', SWAP)]
    all_to_all x0 -> x2, starting transfers between devices: none -> 8.68 us  [exchange(): return lax.all_to_all(parts, axes, 0, 0, tiled=True)]
    pallas_call x0 -> x1, Pallas kernels: none -> 7.97 us  [invert_factor(): pl.pallas_call(invert_factor_kernel, out_shape=jax.ShapeDtypeStruct((RANK...]
  transfers between devices with their start and end apart: 3 -> 5, of which waited for: 3 -> 3; matrix products, arithmetic and copies ran while one was open for 0% -> 3% of each run, Pallas kernels for 0% -> 5%
where the time goes in v1:
time: 158 us; the launch traced here: 157 us
  blocking collectives  82.4 us (52%)
  starting transfers between devices  23.3 us (15%)
  waiting for transfers between devices  21.9 us (14%)
  matrix products  14.3 us (9%)
  Pallas kernels  7.97 us (5%)
  local copies, waits for them, and re-layouts  4.37 us (3%)
  other arithmetic  2.46 us (2%)
    all_to_all x5, blocking collectives, exchange(): return lax.all_to_all(parts, axes, 0, 0, tiled=True)  82.4 us
    all_to_all x2, waiting for transfers between devices, exchange(): return lax.all_to_all(parts, axes, 0, 0, tiled=True)  19.8 us
    dot_general x7, matrix products, dot(): lax.dot_general(a, b, ((contract[0], contract[1]), ((), ())), precision=H...  14.3 us
    all_to_all x2, starting transfers between devices, exchange(): return lax.all_to_all(parts, axes, 0, 0, tiled=True)  8.68 us
    pallas_call x1, Pallas kernels, invert_factor(): pl.pallas_call(invert_factor_kernel, out_shape=jax.ShapeDtypeStruct((RANK...  7.97 us
    ppermute x1, starting transfers between devices, on_device(): gram_theirs = lax.ppermute(gram_mine, 'core', SWAP)  7.09 us
    ppermute x1, starting transfers between devices, on_device(): lax.ppermute(lax.dynamic_index_in_dim(both, 1 - core, 0, False), 'core',...  5.57 us
  transfers between devices with their start and end apart: 5, of which 3 were waited for; matrix products, arithmetic and copies ran while one was open for 3% of the time, Pallas kernels for 5%

profile of v1, /device:TPU:1, one launch (start us, length us, event | category | flops | bytes accessed | tf_op | source)
XLA Modules:
  0.0 157.5 jit_solution(10634747446233908833)
XLA Ops:
  0.6 0.0 copy-start
  0.6 1.3 copy-done
  1.9 2.7 %fusion.12 = f32[256,256]{1,0:T(8,128)S(1)} fusion(f32[1152,256]{1,0:T(8,128)S(1)} %copy-done, f32[256,1152]{1,0:T(8,128)} %param.3, bf16[256,1152]{1,0:T(8,128)(2,1)} %param.4), kind=kOutput, calls=%fused_computation.21 | convolution fusion | flops 906559488 | bytes 3211264 | tf_op jit(solution)/shard_map/dot_general | solution.py:25
  4.6 0.0 copy-start.1
  4.6 30.8 %all_to_all.35 = f32[12,24,256]{2,1,0:T(8,128)S(1)} all-to-all(f32[12,24,256]{2,1,0:T(8,128)S(1)} %bitcast.33), channel_id=1, replica_groups=mesh['x'=4,'y'=8,'core'=2,'col'=12] {'col'}, dimensions={0} | all-to-all | bytes 589824 | tf_op jit(solution)/shard_map/all_to_all | solution.py:31
  35.5 0.7 broadcast_in_dim.14
  36.2 5.0 %all-to-all-start.1 = ((f32[12,24,256]{2,1,0:T(8,128)}), f32[12,24,256]{2,1,0:T(8,128)S(1)}, u32[]{:S(2)}, u32[]{:S(2)}) async-start(f32[12,24,256]{2,1,0:T(8,128)} %broadcast_in_dim.14), calls=%async_computation.1 | async-start | bytes 589824 | tf_op jit(solution)/shard_map/all_to_all | solution.py:31
  41.2 14.2 %all-to-all-done.1 = f32[12,24,256]{2,1,0:T(8,128)S(1)} async-done(((f32[12,24,256]{2,1,0:T(8,128)}), f32[12,24,256]{2,1,0:T(8,128)S(1)}, u32[]{:S(2)}, u32[]{:S(2)}) %all-to-all-start.1) | async-done | bytes 294944 | tf_op jit(solution)/shard_map/all_to_all | solution.py:31
  55.4 0.0 copy-start.3
  55.5 0.7 copy-done.3
  56.2 0.6 fusion.15
  56.8 0.0 copy-done.1
  56.8 0.0 copy-start.5
  56.8 3.2 %fusion.11 = f32[1152,256]{1,0:T(8,128)S(1)} fusion(f32[256,1152]{1,0:T(8,128)S(1)} %copy-done.1, bf16[256,1152]{1,0:T(8,128)(2,1)} %param.4, f32[288,256]{1,0:T(8,128)} %bitcast.28), kind=kOutput, calls=%fused_computation.20 | convolution fusion | flops 906559488 | bytes 3211264 | tf_op jit(solution)/shard_map/dot_general | solution.py:25
  60.0 0.0 copy-done.5
  60.0 0.9 fusion.7
  61.0 5.6 %collective-permute-start = (f32[704,256]{1,0:T(8,128)}, f32[704,256]{1,0:T(8,128)}, u32[]{:S(2)}, u32[]{:S(2)}) collective-permute-start(f32[704,256]{1,0:T(8,128)} %fusion.7), channel_id=1, source_target_pairs={{0,12},{12,0},{1,13},{13,1},{2,14},{14,2},{3,15},{15,3},{4,16},{16... | collective-permute-start | bytes 2162696 | tf_op jit(solution)/shard_map/ppermute | solution.py:139
  66.5 2.1 %collective-permute-done = f32[704,256]{1,0:T(8,128)} collective-permute-done((f32[704,256]{1,0:T(8,128)}, f32[704,256]{1,0:T(8,128)}, u32[]{:S(2)}, u32[]{:S(2)}) %collective-permute-start) | collective-permute-done | bytes 720928 | tf_op jit(solution)/shard_map/ppermute | solution.py:139
  68.7 1.2 fusion.10
  69.9 14.8 %all_to_all.36 = f32[4,176,256]{2,1,0:T(8,128)S(1)} all-to-all(f32[4,176,256]{2,1,0:T(8,128)S(1)} %bitcast.30), channel_id=1, replica_groups=mesh['x'=4,'y'=8,'core'=2,'col'=12] {'x'}, dimensions={0} | all-to-all | bytes 1441792 | tf_op jit(solution)/shard_map/all_to_all | solution.py:31
  84.8 15.3 %all_to_all.37 = f32[8,24,256]{2,1,0:T(8,128)S(1)} all-to-all(f32[8,24,256]{2,1,0:T(8,128)S(1)} %bitcast.34), channel_id=1, replica_groups=mesh['x'=4,'y'=8,'core'=2,'col'=12] {'y'}, dimensions={0} | all-to-all | bytes 393216 | tf_op jit(solution)/shard_map/all_to_all | solution.py:31
  100.2 11.0 %all_to_all.38 = f32[8,24,256]{2,1,0:T(8,128)S(1)} all-to-all(f32[8,24,256]{2,1,0:T(8,128)S(1)} %broadcast_in_dim.15), channel_id=1, replica_groups=mesh['x'=4,'y'=8,'core'=2,'col'=12] {'y'}, dimensions={0} | all-to-all | bytes 393216 | tf_op jit(solution)/shard_map/all_to_all | solution.py:31
  111.2 0.1 broadcast_in_dim.16
  111.3 10.4 %all_to_all.39 = f32[4,176,256]{2,1,0:T(8,128)S(1)} all-to-all(f32[4,176,256]{2,1,0:T(8,128)S(1)} %broadcast_in_dim.16), channel_id=1, replica_groups=mesh['x'=4,'y'=8,'core'=2,'col'=12] {'x'}, dimensions={0} | all-to-all | bytes 1441792 | tf_op jit(solution)/shard_map/all_to_all | solution.py:31
  121.6 7.1 %collective-permute-start.1 = (f32[128,256]{1,0:T(8,128)S(1)}, f32[128,256]{1,0:T(8,128)S(1)}, u32[]{:S(2)}, u32[]{:S(2)}) collective-permute-start(f32[128,256]{1,0:T(8,128)S(1)} %slice.18), channel_id=1, source_target_pairs={{0,12},{12,0},{1,13},{13,1},{2,14},{14,2},{3,15},{15,3},{4,16},{16... | collective-permute-start | bytes 393224 | tf_op jit(solution)/shard_map/ppermute | solution.py:146
  128.8 1.9 %collective-permute-start.2 = (f32[576,256]{1,0:T(8,128)S(1)}, f32[576,256]{1,0:T(8,128)S(1)}, u32[]{:S(2)}, u32[]{:S(2)}) collective-permute-start(f32[576,256]{1,0:T(8,128)S(1)} %slice.19), channel_id=1, source_target_pairs={{0,12},{12,0},{1,13},{13,1},{2,14},{14,2},{3,15},{15,3},{4,16},{16... | collective-permute-start | bytes 1769480 | tf_op jit(solution)/shard_map/ppermute | solution.py:148
  130.7 0.0 collective-permute-done.1
  130.8 0.0 copy-start.4
  130.8 8.0 %invert_factor.1 = f32[256,256]{1,0:T(8,128)S(1)} custom-call(f32[256,256]{1,0:T(8,128)S(1)} %pad_maximum_fusion.gram_ref), custom_call_target="tpu_custom_call" | custom-call | flops 10000000000 | bytes 524288 | tf_op jit(solution)/shard_map/invert_factor/pallas_call | solution.py:119
  138.8 0.0 copy-done.4
  138.8 1.1 fusion.13
  139.9 0.0 collective-permute-done.2
  139.9 0.1 broadcast_select_fusion.1
  140.0 1.1 multiply_reduce_fusion
  141.1 0.6 broadcast_in_dim.17
  141.8 3.7 %all-to-all-start.6 = ((f32[12,1,256]{2,1,0:T(1,128)}), f32[12,1,256]{2,1,0:T(1,128)S(1)}, u32[]{:S(2)}, u32[]{:S(2)}) async-start(f32[12,1,256]{2,1,0:T(1,128)} %broadcast_in_dim.17), calls=%async_computation.6 | async-start | bytes 24576 | tf_op jit(solution)/shard_map/all_to_all | solution.py:31
  145.4 3.4 %fusion = f32[256,1152]{1,0:T(8,128)} fusion(f32[256,256]{1,0:T(8,128)} %fusion.13, f32[1152,256]{1,0:T(8,128)S(1)} %get-tuple-element.8, f32[256,1152]{1,0:T(8,128)S(1)} %copy-done.1, bf16[256,1152]{1,0:T(8,128)(2,1)} %param.4), kind=kOutput, calls=%fused_computation.2 | convolution fusion | flops 907149312 | bytes 4390912 | tf_op jit(solution)/shard_map/dot_general | solution.py:25
  148.9 5.5 %all-to-all-done.6 = f32[12,1,256]{2,1,0:T(1,128)S(1)} async-done(((f32[12,1,256]{2,1,0:T(1,128)}), f32[12,1,256]{2,1,0:T(1,128)S(1)}, u32[]{:S(2)}, u32[]{:S(2)}) %all-to-all-start.6) | async-done | bytes 12320 | tf_op jit(solution)/shard_map/all_to_all | solution.py:31
  154.4 0.0 copy-start.6
  154.5 0.1 broadcast_divide_fusion
  154.6 0.8 copy-done.6
  155.4 0.0 copy-start.2
  155.4 2.1 %fusion.1 = bf16[256,1152]{1,0:T(8,128)(2,1)} fusion(f32[256,256]{1,0:T(8,128)S(1)} %copy-done.6, f32[1152,256]{1,0:T(8,128)S(1)} %broadcast_divide_fusion), kind=kOutput, calls=%fused_computation.3 | convolution fusion | flops 906559488 | bytes 2031616 | tf_op jit(solution)/shard_map/dot_general | solution.py:25
  157.5 0.0 copy-done.2
  (13 shorter events, 0.3 us)
Async XLA Ops:
  0.6 1.3 copy-start
  4.6 52.1 %copy-start.1 = (f32[256,1152]{1,0:T(8,128)S(1)}, f32[256,1152]{1,0:T(8,128)}, u32[]{:S(2)}) copy-start(f32[256,1152]{1,0:T(8,128)} %param.3) | copy-start | bytes 3538948
  36.2 19.2 %all-to-all-start.1 = ((f32[12,24,256]{2,1,0:T(8,128)}), f32[12,24,256]{2,1,0:T(8,128)S(1)}, u32[]{:S(2)}, u32[]{:S(2)}) async-start(f32[12,24,256]{2,1,0:T(8,128)} %broadcast_in_dim.14), calls=%async_computation.1 | async-start | bytes 589824 | tf_op jit(solution)/shard_map/all_to_all | solution.py:31
  55.4 0.7 copy-start.3
  56.8 3.3 %copy-start.5 = (f32[256,256]{1,0:T(8,128)}, f32[256,256]{1,0:T(8,128)S(1)}, u32[]{:S(2)}) copy-start(f32[256,256]{1,0:T(8,128)S(1)} %fusion.15) | copy-start | bytes 786436
  61.0 7.7 %collective-permute-start = (f32[704,256]{1,0:T(8,128)}, f32[704,256]{1,0:T(8,128)}, u32[]{:S(2)}, u32[]{:S(2)}) collective-permute-start(f32[704,256]{1,0:T(8,128)} %fusion.7), channel_id=1, source_target_pairs={{0,12},{12,0},{1,13},{13,1},{2,14},{14,2},{3,15},{15,3},{4,16},{16... | collective-permute-start | bytes 2162696 | tf_op jit(solution)/shard_map/ppermute | solution.py:139
  121.6 9.1 %collective-permute-start.1 = (f32[128,256]{1,0:T(8,128)S(1)}, f32[128,256]{1,0:T(8,128)S(1)}, u32[]{:S(2)}, u32[]{:S(2)}) collective-permute-start(f32[128,256]{1,0:T(8,128)S(1)} %slice.18), channel_id=1, source_target_pairs={{0,12},{12,0},{1,13},{13,1},{2,14},{14,2},{3,15},{15,3},{4,16},{16... | collective-permute-start | bytes 393224 | tf_op jit(solution)/shard_map/ppermute | solution.py:146
  128.8 11.1 %collective-permute-start.2 = (f32[576,256]{1,0:T(8,128)S(1)}, f32[576,256]{1,0:T(8,128)S(1)}, u32[]{:S(2)}, u32[]{:S(2)}) collective-permute-start(f32[576,256]{1,0:T(8,128)S(1)} %slice.19), channel_id=1, source_target_pairs={{0,12},{12,0},{1,13},{13,1},{2,14},{14,2},{3,15},{15,3},{4,16},{16... | collective-permute-start | bytes 1769480 | tf_op jit(solution)/shard_map/ppermute | solution.py:148
  130.8 8.0 %copy-start.4 = (f32[12,24,256]{2,1,0:T(8,128)S(1)}, f32[12,24,256]{2,1,0:T(8,128)}, u32[]{:S(2)}) copy-start(f32[12,24,256]{2,1,0:T(8,128)} %copy-done.3) | copy-start | bytes 884740
  141.8 12.7 %all-to-all-start.6 = ((f32[12,1,256]{2,1,0:T(1,128)}), f32[12,1,256]{2,1,0:T(1,128)S(1)}, u32[]{:S(2)}, u32[]{:S(2)}) async-start(f32[12,1,256]{2,1,0:T(1,128)} %broadcast_in_dim.17), calls=%async_computation.6 | async-start | bytes 24576 | tf_op jit(solution)/shard_map/all_to_all | solution.py:31
  154.4 1.0 copy-start.6
  155.4 2.1 %copy-start.2 = (f32[1152,256]{1,0:T(8,128)}, f32[1152,256]{1,0:T(8,128)S(1)}, u32[]{:S(2)}) copy-start(f32[1152,256]{1,0:T(8,128)S(1)} %broadcast_divide_fusion) | copy-start | bytes 3538948

commit v2 on v1

--- a/solution.py
+++ b/solution.py
@@ -1,3 +1,4 @@
+import functools
 import math
 
 import jax
@@ -27,12 +28,37 @@
     )
 
 
+def call(kernel, shapes, cost, name, limit=16, **more):
+    flops, size = cost
+    return pl.pallas_call(
+        kernel,
+        out_shape=[jax.ShapeDtypeStruct(shape, jnp.float32) for shape in shapes],
+        compiler_params=pltpu.CompilerParams(vmem_limit_bytes=limit << 20),
+        cost_estimate=pl.CostEstimate(flops=flops, bytes_accessed=size, transcendentals=0),
+        name=name,
+        **more,
+    )
+
+
 def exchange(parts, axes):
     return lax.all_to_all(parts, axes, 0, 0, tiled=True)
 
 
 def scatter_sum(parts, axes):
     return jnp.sum(exchange(parts, axes), axis=0)
+
+
+def all_sum(parts, axes, *ready):
+    def kernel(in_ref, out_ref):
+        total = in_ref[0]
+        for i in range(1, in_ref.shape[0]):
+            total = total + in_ref[i]
+        for i in range(in_ref.shape[0]):
+            out_ref[i] = total
+
+    (sums,) = call(kernel, [parts.shape], (10_000_000, 2 * parts.size * 4), "add")(exchange(parts, axes))
+    sums, *ready = lax.optimization_barrier((sums, *ready))
+    return exchange(sums, axes), *ready
 
 
 def gather(part, axes, count):
@@ -88,8 +114,11 @@
     return high, middle, (rest - middle.astype(jnp.float32)).astype(jnp.bfloat16)
 
 
-def invert_factor_kernel(gram_ref, out_ref):
-    out_ref[...] = gram_ref[...]
+def invert_factor_kernel(part_ref, out_ref):
+    out_ref[0:64, 0:128] = part_ref[576:640, 0:128]
+    out_ref[64:128, 0:128] = part_ref[576:640, 128:256]
+    out_ref[0:128, 128:256] = part_ref[640:768, 0:128].T
+    out_ref[128:256, :] = part_ref[640:768, :]
     for low in range(0, RANK, BLOCK):
         high = low + BLOCK
         panel = [out_ref[low + r : low + r + 8, :] for r in range(0, BLOCK, 8)]
@@ -115,52 +144,181 @@
     out_ref[...] = jnp.where(row >= lane, out_ref[...], 0.0)
 
 
-def invert_factor(gram):
+def split2(a):
+    high = a.astype(jnp.bfloat16)
+    return high, (a - high.astype(jnp.float32)).astype(jnp.bfloat16)
+
+
+def dot3(a, b, contract):
+    a_high, a_low = split2(a)
+    b_high, b_low = split2(b)
+    dims = ((contract[0], contract[1]), ((), ()))
+    return (
+        lax.dot_general(a_high, b_low, dims, preferred_element_type=jnp.float32)
+        + lax.dot_general(a_low, b_high, dims, preferred_element_type=jnp.float32)
+    ) + lax.dot_general(a_high, b_high, dims, preferred_element_type=jnp.float32)
+
+
+STEP = 384
+
+
+def left_kernel(product, momentum_hbm, gradient_hbm, factor_hbm, out_ref, momentum_ref, gradient_ref, factor_ref, sems):
+    copies = []
+    for k in range(3):
+        at = pl.ds(k * STEP, STEP)
+        copies.append([
+            pltpu.make_async_copy(momentum_hbm.at[:, at], momentum_ref.at[k], sems.at[k, 0]),
+            pltpu.make_async_copy(factor_hbm.at[at, :], factor_ref.at[k], sems.at[k, 1]),
+            pltpu.make_async_copy(gradient_hbm.at[:, at], gradient_ref.at[k], sems.at[k, 2]),
+        ])
+        for copy in copies[k]:
+            copy.start()
+    out_ref[256:288, :] = jnp.zeros((32, RANK), jnp.float32)
+    total = None
+    for k in range(3):
+        for copy in copies[k]:
+            copy.wait()
+        blended = momentum_ref[k] + gradient_ref[k].astype(jnp.float32)
+        part = product(blended, factor_ref[k], ((1,), (0,)))
+        total = part if total is None else total + part
+    out_ref[0:256, :] = total
+
+
+def left(momentum, gradient, right_factor, product=dot3):
+    hbm = pl.BlockSpec(memory_space=pl.ANY)
     return pl.pallas_call(
-        invert_factor_kernel,
-        out_shape=jax.ShapeDtypeStruct((RANK, RANK), jnp.float32),
-        compiler_params=pltpu.CompilerParams(vmem_limit_bytes=8 << 20),
-        cost_estimate=pl.CostEstimate(flops=10_000_000_000, bytes_accessed=524288, transcendentals=0),
-        name="invert_factor",
-    )(gram)
+        functools.partial(left_kernel, product),
+        in_specs=[hbm] * 3,
+        out_specs=pl.BlockSpec(memory_space=pltpu.VMEM),
+        out_shape=jax.ShapeDtypeStruct((288, RANK), jnp.float32),
+        scratch_shapes=[
+            pltpu.VMEM((3, 256, STEP), jnp.float32),
+            pltpu.VMEM((3, 256, STEP), jnp.bfloat16),
+            pltpu.VMEM((3, STEP, RANK), jnp.float32),
+            pltpu.SemaphoreType.DMA((3, 3)),
+        ],
+        compiler_params=pltpu.CompilerParams(vmem_limit_bytes=60 << 20),
+        cost_estimate=pl.CostEstimate(flops=1_000_000_000, bytes_accessed=3_000_000, transcendentals=0),
+        name="left",
+    )(momentum, gradient, right_factor)
+
+
+def fold_gram(gram):
+    first = jnp.concatenate([gram[0:64, 0:128], gram[64:128, 0:128]], axis=1)
+    return jnp.concatenate([first, gram[128:256, :]], axis=0)
+
+
+def own_sums_kernel(blended_ref, left_ref, out_ref):
+    left = left_ref[0:256, :]
+    out_ref[0:576, :] = dot3(blended_ref[...], left, ((1,), (0,)))
+    out_ref[576:768, :] = fold_gram(dot(left, left, ((0,), (0,))))
+
+
+def other_sums_kernel(own_ref, blended_ref, left_ref, out_ref):
+    left = left_ref[...]
+    out_ref[0:576, :] = own_ref[0:576, :] + dot3(blended_ref[...], left, ((1,), (0,)))
+    out_ref[576:768, :] = own_ref[576:768, :] + fold_gram(dot(left, left, ((0,), (0,))))
+
+
+def right_kernel(core_ref, inverse_ref, left_ref, own_ref, other_ref, out_ref, squares_ref, orthonormal_ref):
+    inverse = inverse_ref[...]
+    own = dot3(own_ref[0:576, :], inverse, ((1,), (1,)))
+    other = dot3(other_ref[...], inverse, ((1,), (1,)))
+    squares = jnp.sum(own * own, axis=0, keepdims=True) + jnp.sum(other * other, axis=0, keepdims=True)
+    squares_ref[...] = jnp.broadcast_to(squares.reshape(1, 1, RANK), (12, 1, RANK))
+
+    orthonormal_ref[...] = dot3(left_ref[0:256, :], inverse, ((1,), (1,)))
+
+    @pl.when(core_ref[0] == 0)
+    def _():
+        out_ref[0:576, :] = own
+        out_ref[576:1152, :] = other
+
+    @pl.when(core_ref[0] == 1)
+    def _():
+        out_ref[0:576, :] = other
+        out_ref[576:1152, :] = own
+
+
+def momentum_kernel(momentum_ref, gradient_ref, orthonormal_ref, right_ref, out_ref):
+    blended = momentum_ref[...] + gradient_ref[...].astype(jnp.float32)
+    product = dot3(orthonormal_ref[...], right_ref[...], ((1,), (1,)))
+    out_ref[...] = blended - (1.0 - decay_rate) * product
+
+
+def feedback(momentum, gradient, orthonormal, right_full):
+    block = pl.BlockSpec((256, STEP), lambda i: (0, i))
+    return call(
+        momentum_kernel, [(256, 1152)], (1_000_000_000, 4_000_000), "momentum",
+        grid=(3,),
+        in_specs=[block, block, pl.BlockSpec((256, RANK), lambda i: (0, 0)), pl.BlockSpec((STEP, RANK), lambda i: (i, 0))],
+        out_specs=[block],
+    )(momentum, gradient, orthonormal, right_full)
+
+
+def update_kernel(product, squares_ref, left_ref, right_ref, new_right_hbm, update_hbm, new_right_ref, update_ref, sems):
+    squares = jnp.sum(squares_ref[...], axis=0)
+    scale = jnp.sqrt(squares + epsilon)
+    factor = math.sqrt(ROWS * COLS / RANK)
+    copies = []
+    for k in range(3):
+        at = pl.ds(k * STEP, STEP)
+        new_right = right_ref[at, :] / scale
+        new_right_ref[at, :] = new_right
+        copies.append(pltpu.make_async_copy(new_right_ref.at[at, :], new_right_hbm.at[at, :], sems.at[k, 0]))
+        copies[-1].start()
+        update_ref[:, at] = (factor * product(left_ref[...], new_right, ((1,), (1,)))).astype(jnp.bfloat16)
+        copies.append(pltpu.make_async_copy(update_ref.at[:, at], update_hbm.at[:, at], sems.at[k, 1]))
+        copies[-1].start()
+    for copy in copies:
+        copy.wait()
+
+
+def last(squares, orthonormal, right_full, product=dot3):
+    vmem = pl.BlockSpec(memory_space=pltpu.VMEM)
+    return pl.pallas_call(
+        functools.partial(update_kernel, product),
+        in_specs=[vmem] * 3,
+        out_specs=[pl.BlockSpec(memory_space=pl.ANY)] * 2,
+        out_shape=[jax.ShapeDtypeStruct((1152, RANK), jnp.float32), jax.ShapeDtypeStruct((256, 1152), jnp.bfloat16)],
+        scratch_shapes=[
+            pltpu.VMEM((1152, RANK), jnp.float32),
+            pltpu.VMEM((256, 1152), jnp.bfloat16),
+            pltpu.SemaphoreType.DMA((3, 2)),
+        ],
+        compiler_params=pltpu.CompilerParams(vmem_limit_bytes=16 << 20),
+        cost_estimate=pl.CostEstimate(flops=1_000_000_000, bytes_accessed=3_000_000, transcendentals=0),
+        name="update",
+    )(squares, orthonormal, right_full)
 
 
 def on_device(momentum, gradient, right_factor):
     core = lax.axis_index("core")
+    left_parts = left(momentum, gradient, right_factor)
     blended = momentum + gradient.astype(jnp.float32)
-    left_local = dot(blended, right_factor, ((1,), (0,)))
-    left_parts = jnp.pad(left_local, ((0, 32), (0, 0))).reshape(12, 24, RANK)
-    left_raw = gather(scatter_sum(left_parts, "col"), "col", 12).reshape(288, RANK)[:256]
-
-    gram_local = dot(left_raw, left_raw, ((0,), (0,))).reshape(2, 128, RANK)
-    right_local = dot(blended, left_raw, ((0,), (0,))).reshape(2, 576, RANK)
-    both = jnp.concatenate([right_local, gram_local], axis=1)
-    mine = lax.dynamic_index_in_dim(both, core, 0, False)
-    theirs = lax.ppermute(lax.dynamic_index_in_dim(both, 1 - core, 0, False), "core", SWAP)
-    part = scatter_sum((mine + theirs).reshape(4, 176, RANK), "x")
-    part = scatter_sum(jnp.pad(part, ((0, 16), (0, 0))).reshape(8, 24, RANK), "y")
-    part = gather(part, "y", 8).reshape(192, RANK)[:176]
-    part = gather(part, "x", 4).reshape(704, RANK)
-
-    gram_mine = part[576:]
-    gram_theirs = lax.ppermute(gram_mine, "core", SWAP)
-    right_mine = part[:576]
-    right_theirs = lax.ppermute(right_mine, "core", SWAP)
-
-    def in_order(own, other):
-        return jnp.concatenate([jnp.where(core == 0, own, other), jnp.where(core == 0, other, own)], axis=0)
-
-    inverse = invert_factor(in_order(gram_mine, gram_theirs))
-    right_raw = in_order(right_mine, right_theirs)
-    orthonormal = dot(left_raw, inverse, ((1,), (1,)))
-    right_full = dot(right_raw, inverse, ((1,), (1,)))
-    squares = jnp.sum(right_full * right_full, axis=0, keepdims=True)
-    squares = jnp.sum(gather(squares, "col", 12), axis=(0, 1))
-
-    new_momentum = blended - (1.0 - decay_rate) * dot(orthonormal, right_full, ((1,), (1,)))
-    new_right = right_full / jnp.sqrt(squares + epsilon)
-    factor = math.sqrt(ROWS * COLS / RANK)
-    update = (factor * dot(orthonormal, new_right, ((1,), (1,)))).astype(jnp.bfloat16)
+    kept = lax.dynamic_slice(blended, (0, core * 576), (256, 576))
+    sent = lax.dynamic_slice(blended, (0, (1 - core) * 576), (256, 576))
+    taken = lax.ppermute(sent, "core", SWAP)
+    left_own, kept, taken = all_sum(left_parts.reshape(12, 24, RANK), "col", kept.T, taken.T)
+    left_own = left_own.reshape(288, RANK)
+    left_other = lax.ppermute(left_own[:256], "core", SWAP)
+    cost = (500_000_000, 3_000_000)
+    (own,) = call(own_sums_kernel, [(768, RANK)], cost, "own_sums")(kept, left_own)
+    (sums,) = call(other_sums_kernel, [(768, RANK)], cost, "other_sums")(own, taken, left_other)
+    part = scatter_sum(sums.reshape(4, 192, RANK), "x")
+    (part,) = all_sum(part.reshape(8, 24, RANK), "y")
+    part = part.reshape(192, RANK)
+    part = gather(part, "x", 4).reshape(768, RANK)
+
+    right_theirs = lax.ppermute(part[:576], "core", SWAP)
+    (inverse,) = call(invert_factor_kernel, [(RANK, RANK)], (10_000_000_000, 524288), "inverse")(part)
+    right_full, squares, orthonormal = call(
+        right_kernel, [(1152, RANK), (12, 1, RANK), (256, RANK)], (1_000_000_000, 3_000_000), "right",
+        in_specs=[pl.BlockSpec(memory_space=pltpu.SMEM)] + [pl.BlockSpec(memory_space=pltpu.VMEM)] * 4,
+    )(core.reshape(1), inverse, left_own, part, right_theirs)
+    squares = exchange(squares, "col")
+    (new_momentum,) = feedback(momentum, gradient, orthonormal, right_full)
+    new_right, update = last(squares, orthonormal, right_full)
     return (new_momentum, new_right, update)
 
 

time: 158 us -> 145 us (0.918)
  matrix products: 14.3 us -> 0 us
  starting transfers between devices: 23.3 us -> 34 us
  Pallas kernels: 7.97 us -> 18.1 us
  blocking collectives: 82.4 us -> 72.5 us
  waiting for transfers between devices: 21.9 us -> 14.1 us
    dot_general x7 -> x0, matrix products: 14.3 us -> none  [dot(): lax.dot_general(a, b, ((contract[0], contract[1]), ((), ())), precision=H...]
    all_to_all x2, starting transfers between devices: 8.68 us -> 19.2 us  [exchange(): return lax.all_to_all(parts, axes, 0, 0, tiled=True)]
    pallas_call x1 -> x9, Pallas kernels: 7.97 us -> 18.1 us  [the longest x1 7.99 us: on_device(): call(invert_factor_kernel, [(RANK, RANK)], (10000000000, 524288), 'inverse')]
    all_to_all x5, blocking collectives: 82.4 us -> 72.5 us  [exchange(): return lax.all_to_all(parts, axes, 0, 0, tiled=True)]
    all_to_all x2, waiting for transfers between devices: 19.8 us -> 13.6 us  [exchange(): return lax.all_to_all(parts, axes, 0, 0, tiled=True)]
    ppermute x3, waiting for transfers between devices: 2.14 us -> 0.48 us  [the longest x1 0.47 us: on_device(): left_other = lax.ppermute(left_own[:256], 'core', SWAP)]
  transfers between devices with their start and end apart: 5 -> 5, of which waited for: 3 -> 3; matrix products, arithmetic and copies ran while one was open for 3% -> 4% of each run, Pallas kernels for 5% -> 8%
where the time goes in v2:
time: 145 us
  blocking collectives  72.5 us (50%)
  starting transfers between devices  34 us (23%)
  Pallas kernels  18.1 us (12%)
  waiting for transfers between devices  14.1 us (10%)
  local copies, waits for them, and re-layouts  3.68 us (3%)
  other arithmetic  1.59 us (1%)
    all_to_all x5, blocking collectives, exchange(): return lax.all_to_all(parts, axes, 0, 0, tiled=True)  72.5 us
    all_to_all x2, starting transfers between devices, exchange(): return lax.all_to_all(parts, axes, 0, 0, tiled=True)  19.2 us
    all_to_all x2, waiting for transfers between devices, exchange(): return lax.all_to_all(parts, axes, 0, 0, tiled=True)  13.6 us
    pallas_call x1, Pallas kernels, on_device(): call(invert_factor_kernel, [(RANK, RANK)], (10000000000, 524288), 'inverse')  7.99 us
    ppermute x1, starting transfers between devices, on_device(): right_theirs = lax.ppermute(part[:576], 'core', SWAP)  7.3 us
    ppermute x1, starting transfers between devices, on_device(): left_other = lax.ppermute(left_own[:256], 'core', SWAP)  4.65 us
    pallas_call x1, Pallas kernels, left(): pl.pallas_call(functools.partial(left_kernel, product), in_specs=[hbm] *...  3.32 us
  transfers between devices with their start and end apart: 5, of which 3 were waited for; matrix products, arithmetic and copies ran while one was open for 4% of the time, Pallas kernels for 8%

profile of v2, /device:TPU:1, one launch (start us, length us, event | category | flops | bytes accessed | tf_op | source)
XLA Modules:
  0.0 144.8 jit_solution(15713990135379994578)
XLA Ops:
  0.6 0.0 copy-start
  0.6 3.3 %left.1 = f32[288,256]{1,0:T(8,128)} custom-call(f32[256,1152]{1,0:T(8,128)} %momentum_ref.1, bf16[256,1152]{1,0:T(8,128)(2,1)} %gradient_ref.1, f32[1152,256]{1,0:T(8,128)} %factor_hbm.1), custom_call_target="tpu_custom_call" | custom-call | flops 1000000000 | bytes 3000000 | tf_op jit(solution)/shard_map/left/pallas_call | solution.py:189
  4.0 15.7 %all-to-all-start = ((f32[12,24,256]{2,1,0:T(8,128)}), f32[12,24,256]{2,1,0:T(8,128)S(1)}, u32[]{:S(2)}, u32[]{:S(2)}) async-start(f32[12,24,256]{2,1,0:T(8,128)} %bitcast.21), calls=%async_computation | async-start | bytes 589824 | tf_op jit(solution)/shard_map/all_to_all | solution.py:44
  19.7 0.0 copy-done
  19.7 0.0 copy-start.1
  19.7 1.4 copy.7
  21.1 0.0 copy-done.1
  21.1 1.1 copy.6
  22.2 1.5 %convert_add_fusion = f32[256,1152]{0,1:T(8,128)S(1)} fusion(f32[256,1152]{0,1:T(8,128)} %copy.7, bf16[256,1152]{0,1:T(8,128)(2,1)} %copy.6), kind=kLoop, calls=%fused_computation | loop fusion | flops 589824 | bytes 2949120 | tf_op jit(solution)/shard_map/add | solution.py:298
  23.7 1.1 constant_dynamic-slice_fusion
  24.8 2.9 %collective-permute-start = (f32[256,576]{0,1:T(8,128)}, f32[256,576]{0,1:T(8,128)S(1)}, u32[]{:S(2)}, u32[]{:S(2)}) collective-permute-start(f32[256,576]{0,1:T(8,128)} %get-tuple-element.19), channel_id=1, source_target_pairs={{0,12},{12,0},{1,13},{13,1},{2,14},{14,2},{3,15},{15,3},{4,16},{16... | collective-permute-start | bytes 1769480 | tf_op jit(solution)/shard_map/ppermute | solution.py:301
  27.7 7.2 %all-to-all-done.in_ref = f32[12,24,256]{2,1,0:T(8,128)S(1)} async-done(((f32[12,24,256]{2,1,0:T(8,128)}), f32[12,24,256]{2,1,0:T(8,128)S(1)}, u32[]{:S(2)}, u32[]{:S(2)}) %all-to-all-start) | async-done | bytes 294944 | tf_op jit(solution)/shard_map/all_to_all | solution.py:44
  34.8 0.0 copy-start.2
  34.9 0.0 collective-permute-done
  34.9 0.0 copy-start.3
  34.9 20.1 %all_to_all.35 = f32[12,24,256]{2,1,0:T(8,128)S(1)} all-to-all(f32[12,24,256]{2,1,0:T(8,128)S(1)} %add.15), channel_id=1, replica_groups=mesh['x'=4,'y'=8,'core'=2,'col'=12] {'col'}, dimensions={0} | all-to-all | bytes 589824 | tf_op jit(solution)/shard_map/all_to_all | solution.py:44
  55.0 0.0 copy-done.3
  55.0 4.7 %collective-permute-start.1 = (f32[256,256]{1,0:T(8,128)S(1)}, f32[256,256]{1,0:T(8,128)S(1)}, u32[]{:S(2)}, u32[]{:S(2)}) collective-permute-start(f32[256,256]{1,0:T(8,128)S(1)} %slice.12), channel_id=1, source_target_pairs={{0,12},{12,0},{1,13},{13,1},{2,14},{14,2},{3,15},{15,3},{4,16},{16... | collective-permute-start | bytes 786440 | tf_op jit(solution)/shard_map/ppermute | solution.py:304
  59.7 0.0 copy-done.2
  59.7 0.0 copy-start.4
  59.7 0.6 own_sums.1.own_ref
  60.4 0.5 collective-permute-done.1.left_ref
  60.8 0.0 copy-done.4
  60.8 0.6 other_sums.1
  61.5 15.2 %all_to_all.36 = f32[4,192,256]{2,1,0:T(8,128)S(1)} all-to-all(f32[4,192,256]{2,1,0:T(8,128)S(1)} %bitcast.11), channel_id=1, replica_groups=mesh['x'=4,'y'=8,'core'=2,'col'=12] {'x'}, dimensions={0} | all-to-all | bytes 1572864 | tf_op jit(solution)/shard_map/all_to_all | solution.py:44
  76.7 0.1 reduce_sum.9
  76.8 15.3 %all_to_all.37.in_ref = f32[8,24,256]{2,1,0:T(8,128)S(1)} all-to-all(f32[8,24,256]{2,1,0:T(8,128)S(1)} %bitcast.18), channel_id=1, replica_groups=mesh['x'=4,'y'=8,'core'=2,'col'=12] {'y'}, dimensions={0} | all-to-all | bytes 393216 | tf_op jit(solution)/shard_map/all_to_all | solution.py:44
  92.1 11.1 %all_to_all.38 = f32[8,24,256]{2,1,0:T(8,128)S(1)} all-to-all(f32[8,24,256]{2,1,0:T(8,128)S(1)} %add.16), channel_id=1, replica_groups=mesh['x'=4,'y'=8,'core'=2,'col'=12] {'y'}, dimensions={0} | all-to-all | bytes 393216 | tf_op jit(solution)/shard_map/all_to_all | solution.py:44
  103.2 0.1 broadcast_in_dim.3
  103.3 10.7 %all_to_all.39 = f32[4,192,256]{2,1,0:T(8,128)S(1)} all-to-all(f32[4,192,256]{2,1,0:T(8,128)S(1)} %broadcast_in_dim.3), channel_id=1, replica_groups=mesh['x'=4,'y'=8,'core'=2,'col'=12] {'x'}, dimensions={0} | all-to-all | bytes 1572864 | tf_op jit(solution)/shard_map/all_to_all | solution.py:44
  114.1 7.3 %collective-permute-start.2 = (f32[576,256]{1,0:T(8,128)S(1)}, f32[576,256]{1,0:T(8,128)S(1)}, u32[]{:S(2)}, u32[]{:S(2)}) collective-permute-start(f32[576,256]{1,0:T(8,128)S(1)} %bitcast.20), channel_id=1, source_target_pairs={{0,12},{12,0},{1,13},{13,1},{2,14},{14,2},{3,15},{15,3},{4,16},{16... | collective-permute-start | bytes 1769480 | tf_op jit(solution)/shard_map/ppermute | solution.py:313
  121.4 8.0 %inverse.1.inverse_ref = f32[256,256]{1,0:T(8,128)S(1)} custom-call(f32[768,256]{1,0:T(8,128)S(1)} %bitcast.12), custom_call_target="tpu_custom_call" | custom-call | flops 10000000000 | bytes 524288 | tf_op jit(solution)/shard_map/inverse/pallas_call | solution.py:314
  129.4 0.0 collective-permute-done.2.other_ref
  129.4 1.5 %right.1 = (f32[1152,256]{1,0:T(8,128)S(1)}, f32[12,1,256]{2,1,0:T(1,128)}, f32[256,256]{1,0:T(8,128)S(1)}) custom-call(s32[1]{0:T(128)} %bitcast.core_ref, f32[256,256]{1,0:T(8,128)S(1)} %inverse.1.inverse_ref, f32[288,256]{1,0:T(8,128)S(1)} %bitcast.16, f32[768,256]{1,0:T(8,128)S(1)} %bitcast.13, f32[576,256]{1,0:T(8,128)S(1)} %collective-permute-done.2.other_ref), custom_call_target="tpu_custom_call" | custom-call | flops 1000000000 | bytes 3000000 | tf_op jit(solution)/shard_map/right/pallas_call | solution.py:315
  130.8 3.5 %all-to-all-start.6 = ((f32[12,1,256]{2,1,0:T(1,128)}), f32[12,1,256]{2,1,0:T(1,128)S(1)}, u32[]{:S(2)}, u32[]{:S(2)}) async-start(f32[12,1,256]{2,1,0:T(1,128)} %get-tuple-element.16), calls=%async_computation.6 | async-start | bytes 24576 | tf_op jit(solution)/shard_map/all_to_all | solution.py:44
  134.3 2.4 %momentum.1 = f32[256,1152]{1,0:T(8,128)} custom-call(f32[256,1152]{1,0:T(8,128)S(1)} %copy-done, bf16[256,1152]{1,0:T(8,128)(2,1)S(1)} %copy-done.1, f32[256,256]{1,0:T(8,128)S(1)} %get-tuple-element.14.orthonormal_ref.left_ref, f32[1152,256]{1,0:T(8,128)S(1)} %get-tuple-element.15.right_ref), custom_call_target="tpu_custom_call" | custom-call | flops 1000000000 | bytes 4000000 | tf_op jit(solution)/shard_map/momentum/pallas_call | solution.py:251
  136.8 6.5 %all-to-all-done.6.squares_ref = f32[12,1,256]{2,1,0:T(1,128)S(1)} async-done(((f32[12,1,256]{2,1,0:T(1,128)}), f32[12,1,256]{2,1,0:T(1,128)S(1)}, u32[]{:S(2)}, u32[]{:S(2)}) %all-to-all-start.6) | async-done | bytes 12320 | tf_op jit(solution)/shard_map/all_to_all | solution.py:44
  143.2 1.6 %update.1 = (f32[1152,256]{1,0:T(8,128)}, bf16[256,1152]{1,0:T(8,128)(2,1)}) custom-call(f32[12,1,256]{2,1,0:T(1,128)S(1)} %all-to-all-done.6.squares_ref, f32[256,256]{1,0:T(8,128)S(1)} %get-tuple-element.14.orthonormal_ref.left_ref, f32[1152,256]{1,0:T(8,128)S(1)} %get-tuple-element.15.right_ref), custom_call_target="tpu_custom_call" | custom-call | flops 1000000000 | bytes 3000000 | tf_op jit(solution)/shard_map/update/pallas_call | solution.py:279
  (4 shorter events, 0.1 us)
Async XLA Ops:
  0.6 19.1 %copy-start = (f32[256,1152]{1,0:T(8,128)S(1)}, f32[256,1152]{1,0:T(8,128)}, u32[]{:S(2)}) copy-start(f32[256,1152]{1,0:T(8,128)} %momentum_ref.1) | copy-start | bytes 3538948
  4.0 30.9 %all-to-all-start = ((f32[12,24,256]{2,1,0:T(8,128)}), f32[12,24,256]{2,1,0:T(8,128)S(1)}, u32[]{:S(2)}, u32[]{:S(2)}) async-start(f32[12,24,256]{2,1,0:T(8,128)} %bitcast.21), calls=%async_computation | async-start | bytes 589824 | tf_op jit(solution)/shard_map/all_to_all | solution.py:44
  19.7 1.4 copy-start.1
  24.8 10.1 %collective-permute-start = (f32[256,576]{0,1:T(8,128)}, f32[256,576]{0,1:T(8,128)S(1)}, u32[]{:S(2)}, u32[]{:S(2)}) collective-permute-start(f32[256,576]{0,1:T(8,128)} %get-tuple-element.19), channel_id=1, source_target_pairs={{0,12},{12,0},{1,13},{13,1},{2,14},{14,2},{3,15},{15,3},{4,16},{16... | collective-permute-start | bytes 1769480 | tf_op jit(solution)/shard_map/ppermute | solution.py:301
  34.8 24.8 %copy-start.2 = (f32[576,256]{1,0:T(8,128)S(1)}, f32[576,256]{1,0:T(8,128)}, u32[]{:S(2)}) copy-start(f32[576,256]{1,0:T(8,128)} %get-tuple-element.11.blended_ref) | copy-start | bytes 1769476
  34.9 20.1 %copy-start.3 = (f32[256,576]{0,1:T(8,128)}, f32[256,576]{0,1:T(8,128)S(1)}, u32[]{:S(2)}) copy-start(f32[256,576]{0,1:T(8,128)S(1)} %collective-permute-done) | copy-start | bytes 1769476
  55.0 5.8 %collective-permute-start.1 = (f32[256,256]{1,0:T(8,128)S(1)}, f32[256,256]{1,0:T(8,128)S(1)}, u32[]{:S(2)}, u32[]{:S(2)}) collective-permute-start(f32[256,256]{1,0:T(8,128)S(1)} %slice.12), channel_id=1, source_target_pairs={{0,12},{12,0},{1,13},{13,1},{2,14},{14,2},{3,15},{15,3},{4,16},{16... | collective-permute-start | bytes 786440 | tf_op jit(solution)/shard_map/ppermute | solution.py:304
  59.7 1.1 copy-start.4
  114.1 15.3 %collective-permute-start.2 = (f32[576,256]{1,0:T(8,128)S(1)}, f32[576,256]{1,0:T(8,128)S(1)}, u32[]{:S(2)}, u32[]{:S(2)}) collective-permute-start(f32[576,256]{1,0:T(8,128)S(1)} %bitcast.20), channel_id=1, source_target_pairs={{0,12},{12,0},{1,13},{13,1},{2,14},{14,2},{3,15},{15,3},{4,16},{16... | collective-permute-start | bytes 1769480 | tf_op jit(solution)/shard_map/ppermute | solution.py:313
  130.8 12.4 %all-to-all-start.6 = ((f32[12,1,256]{2,1,0:T(1,128)}), f32[12,1,256]{2,1,0:T(1,128)S(1)}, u32[]{:S(2)}, u32[]{:S(2)}) async-start(f32[12,1,256]{2,1,0:T(1,128)} %get-tuple-element.16), calls=%async_computation.6 | async-start | bytes 24576 | tf_op jit(solution)/shard_map/all_to_all | solution.py:44

commit v3 on v2

--- a/solution.py
+++ b/solution.py
@@ -72,39 +72,46 @@
 def invert_panel(panel, low):
     pieces = len(panel)
     row8 = lax.broadcasted_iota(jnp.int32, (8, 128), 0)
-    lane = lax.broadcasted_iota(jnp.int32, (8, 128), 1)
-    unit = [(row8 + 8 * r == lane).astype(jnp.float32) for r in range(pieces)]
+    row = lax.broadcasted_iota(jnp.int32, (8, RANK), 0)
+    place = lax.broadcasted_iota(jnp.int32, (8, RANK), 1)
     scales = []
+
+    def spread(group, start):
+        return [
+            [
+                jnp.broadcast_to(panel[r][:, at : at + 1], (8, 128)) if r >= start else None for r in range(pieces)
+            ]
+            for at in range(low + 8 * group, low + 8 * group + 8)
+        ]
+
+    ahead = None
     for g in range(pieces):
-        columns = []
-        for i in range(8):
-            at = low + 8 * g + i
-            columns.append([
-                jnp.broadcast_to(panel[r][:, at : at + 1], (8, 128)) if r >= g else None for r in range(pieces)
-            ])
+        columns = ahead or spread(g, g)
+        ahead = spread(g + 1, g) if g < pieces - 1 else None
+        at = low + 8 * g
+        inside = (place >= at) & (place < at + 8)
+        for r in range(pieces):
+            panel[r] = jnp.where(inside, jnp.where(place == row + at, 1.0, 0.0) if r == g else 0.0, panel[r])
         pivots = jnp.zeros((8, 128), jnp.float32)
-        factors = []
         for i in range(8):
             pivot = columns[i][g][i : i + 1, :]
             pivots = jnp.where(row8 == i, pivot, pivots)
             inverse = 1.0 / pivot
             factor = [columns[i][r] * inverse if r >= g else None for r in range(pieces)]
             factor[g] = jnp.where(row8 > i, factor[g], 0.0)
-            factors.append(factor)
+            panel_row = jnp.broadcast_to(panel[g][i : i + 1, :], (8, RANK))
+            for r in range(g, pieces):
+                panel[r] = panel[r] - wide(factor[r]) * panel_row
+            for column in ahead or []:
+                head = column[g][i : i + 1, :]
+                for r in range(g, pieces):
+                    column[r] = column[r] - factor[r] * head
             for l in range(i + 1, 8):
                 head = columns[l][g][i : i + 1, :]
                 for r in range(g, pieces):
                     columns[l][r] = columns[l][r] - factor[r] * head
-        for i in range(8):
-            panel_row = panel[g][i : i + 1, :]
-            unit_row = unit[g][i : i + 1, :]
-            for r in range(g, pieces):
-                panel[r] = panel[r] - wide(factors[i][r]) * panel_row
-                unit[r] = unit[r] - factors[i][r] * unit_row
         scales.append(lax.rsqrt(pivots))
-    panel = [panel[r] * wide(scales[r]) for r in range(pieces)]
-    unit = [unit[r] * scales[r] for r in range(pieces)]
-    return panel, unit
+    return [panel[r] * wide(scales[r]) for r in range(pieces)]
 
 
 def split3(a):
@@ -122,9 +129,8 @@
     for low in range(0, RANK, BLOCK):
         high = low + BLOCK
         panel = [out_ref[low + r : low + r + 8, :] for r in range(0, BLOCK, 8)]
-        panel, unit = invert_panel(panel, low)
+        panel = invert_panel(panel, low)
         out_ref[low:high, :] = jnp.concatenate(panel, axis=0)
-        out_ref[low:high, low:high] = jnp.concatenate(unit, axis=0)[:, :BLOCK]
         if high < RANK:
             left = RANK - high
             a, b, c = split3(out_ref[low:high, :])
@@ -220,13 +226,16 @@
     out_ref[576:768, :] = own_ref[576:768, :] + fold_gram(dot(left, left, ((0,), (0,))))
 
 
-def right_kernel(core_ref, inverse_ref, left_ref, own_ref, other_ref, out_ref, squares_ref, orthonormal_ref):
+def right_kernel(
+    core_ref, inverse_ref, left_ref, own_ref, other_ref, out_ref, orthonormal_ref, squares_hbm, squares_ref, sem
+):
     inverse = inverse_ref[...]
     own = dot3(own_ref[0:576, :], inverse, ((1,), (1,)))
     other = dot3(other_ref[...], inverse, ((1,), (1,)))
     squares = jnp.sum(own * own, axis=0, keepdims=True) + jnp.sum(other * other, axis=0, keepdims=True)
     squares_ref[...] = jnp.broadcast_to(squares.reshape(1, 1, RANK), (12, 1, RANK))
-
+    copy = pltpu.make_async_copy(squares_ref, squares_hbm, sem)
+    copy.start()
     orthonormal_ref[...] = dot3(left_ref[0:256, :], inverse, ((1,), (1,)))
 
     @pl.when(core_ref[0] == 0)
@@ -238,6 +247,8 @@
     def _():
         out_ref[0:576, :] = other
         out_ref[576:1152, :] = own
+
+    copy.wait()
 
 
 def momentum_kernel(momentum_ref, gradient_ref, orthonormal_ref, right_ref, out_ref):
@@ -312,9 +323,12 @@
 
     right_theirs = lax.ppermute(part[:576], "core", SWAP)
     (inverse,) = call(invert_factor_kernel, [(RANK, RANK)], (10_000_000_000, 524288), "inverse")(part)
-    right_full, squares, orthonormal = call(
-        right_kernel, [(1152, RANK), (12, 1, RANK), (256, RANK)], (1_000_000_000, 3_000_000), "right",
-        in_specs=[pl.BlockSpec(memory_space=pltpu.SMEM)] + [pl.BlockSpec(memory_space=pltpu.VMEM)] * 4,
+    vmem = pl.BlockSpec(memory_space=pltpu.VMEM)
+    right_full, orthonormal, squares = call(
+        right_kernel, [(1152, RANK), (256, RANK), (12, 1, RANK)], (1_000_000_000, 3_000_000), "right",
+        in_specs=[pl.BlockSpec(memory_space=pltpu.SMEM)] + [vmem] * 4,
+        out_specs=[vmem, vmem, pl.BlockSpec(memory_space=pl.ANY)],
+        scratch_shapes=[pltpu.VMEM((12, 1, RANK), jnp.float32), pltpu.SemaphoreType.DMA],
     )(core.reshape(1), inverse, left_own, part, right_theirs)
     squares = exchange(squares, "col")
     (new_momentum,) = feedback(momentum, gradient, orthonormal, right_full)

time: 145 us -> 144 us (level)
  Pallas kernels: 18.1 us -> 16.3 us
    pallas_call x1, Pallas kernels: 7.99 us -> 6.21 us  [on_device(): call(invert_factor_kernel, [(RANK, RANK)], (10000000000, 524288), 'inverse')]
  transfers between devices with their start and end apart: 5 -> 5, of which waited for: 3 -> 3; matrix products, arithmetic and copies ran while one was open for 4% -> 4% of each run, Pallas kernels for 8% -> 7%
where the time goes in v3:
time: 144 us; the launch traced here: 143 us
  blocking collectives  72.5 us (50%)
  starting transfers between devices  34 us (24%)
  Pallas kernels  16.3 us (11%)
  waiting for transfers between devices  14.1 us (10%)
  local copies, waits for them, and re-layouts  3.68 us (3%)
  other arithmetic  1.59 us (1%)
    all_to_all x5, blocking collectives, exchange(): return lax.all_to_all(parts, axes, 0, 0, tiled=True)  72.5 us
    all_to_all x2, starting transfers between devices, exchange(): return lax.all_to_all(parts, axes, 0, 0, tiled=True)  19.2 us
    all_to_all x2, waiting for transfers between devices, exchange(): return lax.all_to_all(parts, axes, 0, 0, tiled=True)  13.6 us
    ppermute x1, starting transfers between devices, on_device(): right_theirs = lax.ppermute(part[:576], 'core', SWAP)  7.3 us
    pallas_call x1, Pallas kernels, on_device(): call(invert_factor_kernel, [(RANK, RANK)], (10000000000, 524288), 'inverse')  6.21 us
    ppermute x1, starting transfers between devices, on_device(): left_other = lax.ppermute(left_own[:256], 'core', SWAP)  4.65 us
    pallas_call x1, Pallas kernels, left(): pl.pallas_call(functools.partial(left_kernel, product), in_specs=[hbm] *...  3.32 us
  transfers between devices with their start and end apart: 5, of which 3 were waited for; matrix products, arithmetic and copies ran while one was open for 4% of the time, Pallas kernels for 7%

profile of v3, /device:TPU:1, one launch (start us, length us, event | category | flops | bytes accessed | tf_op | source)
XLA Modules:
  0.0 143.0 jit_solution(13065202823143703882)
XLA Ops:
  0.6 0.0 copy-start
  0.6 3.3 %left.1 = f32[288,256]{1,0:T(8,128)} custom-call(f32[256,1152]{1,0:T(8,128)} %momentum_ref.1, bf16[256,1152]{1,0:T(8,128)(2,1)} %gradient_ref.1, f32[1152,256]{1,0:T(8,128)} %factor_hbm.1), custom_call_target="tpu_custom_call" | custom-call | flops 1000000000 | bytes 3000000 | tf_op jit(solution)/shard_map/left/pallas_call | solution.py:195
  4.0 15.7 %all-to-all-start = ((f32[12,24,256]{2,1,0:T(8,128)}), f32[12,24,256]{2,1,0:T(8,128)S(1)}, u32[]{:S(2)}, u32[]{:S(2)}) async-start(f32[12,24,256]{2,1,0:T(8,128)} %bitcast.21), calls=%async_computation | async-start | bytes 589824 | tf_op jit(solution)/shard_map/all_to_all | solution.py:44
  19.7 0.0 copy-done
  19.7 0.0 copy-start.1
  19.7 1.4 copy.7
  21.1 0.0 copy-done.1
  21.1 1.1 copy.6
  22.2 1.5 %convert_add_fusion = f32[256,1152]{0,1:T(8,128)S(1)} fusion(f32[256,1152]{0,1:T(8,128)} %copy.7, bf16[256,1152]{0,1:T(8,128)(2,1)} %copy.6), kind=kLoop, calls=%fused_computation | loop fusion | flops 589824 | bytes 2949120 | tf_op jit(solution)/shard_map/add | solution.py:309
  23.7 1.1 constant_dynamic-slice_fusion
  24.8 2.9 %collective-permute-start = (f32[256,576]{0,1:T(8,128)}, f32[256,576]{0,1:T(8,128)S(1)}, u32[]{:S(2)}, u32[]{:S(2)}) collective-permute-start(f32[256,576]{0,1:T(8,128)} %get-tuple-element.19), channel_id=1, source_target_pairs={{0,12},{12,0},{1,13},{13,1},{2,14},{14,2},{3,15},{15,3},{4,16},{16... | collective-permute-start | bytes 1769480 | tf_op jit(solution)/shard_map/ppermute | solution.py:312
  27.7 7.2 %all-to-all-done.in_ref = f32[12,24,256]{2,1,0:T(8,128)S(1)} async-done(((f32[12,24,256]{2,1,0:T(8,128)}), f32[12,24,256]{2,1,0:T(8,128)S(1)}, u32[]{:S(2)}, u32[]{:S(2)}) %all-to-all-start) | async-done | bytes 294944 | tf_op jit(solution)/shard_map/all_to_all | solution.py:44
  34.8 0.0 copy-start.2
  34.9 0.0 collective-permute-done
  34.9 0.0 copy-start.3
  34.9 20.1 %all_to_all.35 = f32[12,24,256]{2,1,0:T(8,128)S(1)} all-to-all(f32[12,24,256]{2,1,0:T(8,128)S(1)} %add.15), channel_id=1, replica_groups=mesh['x'=4,'y'=8,'core'=2,'col'=12] {'col'}, dimensions={0} | all-to-all | bytes 589824 | tf_op jit(solution)/shard_map/all_to_all | solution.py:44
  55.0 0.0 copy-done.3
  55.0 4.7 %collective-permute-start.1 = (f32[256,256]{1,0:T(8,128)S(1)}, f32[256,256]{1,0:T(8,128)S(1)}, u32[]{:S(2)}, u32[]{:S(2)}) collective-permute-start(f32[256,256]{1,0:T(8,128)S(1)} %slice.12), channel_id=1, source_target_pairs={{0,12},{12,0},{1,13},{13,1},{2,14},{14,2},{3,15},{15,3},{4,16},{16... | collective-permute-start | bytes 786440 | tf_op jit(solution)/shard_map/ppermute | solution.py:315
  59.7 0.0 copy-done.2
  59.7 0.0 copy-start.4
  59.7 0.6 own_sums.1.own_ref
  60.4 0.5 collective-permute-done.1.left_ref
  60.8 0.0 copy-done.4
  60.8 0.6 other_sums.1
  61.5 15.2 %all_to_all.36 = f32[4,192,256]{2,1,0:T(8,128)S(1)} all-to-all(f32[4,192,256]{2,1,0:T(8,128)S(1)} %bitcast.11), channel_id=1, replica_groups=mesh['x'=4,'y'=8,'core'=2,'col'=12] {'x'}, dimensions={0} | all-to-all | bytes 1572864 | tf_op jit(solution)/shard_map/all_to_all | solution.py:44
  76.7 0.1 reduce_sum.9
  76.8 15.3 %all_to_all.37.in_ref = f32[8,24,256]{2,1,0:T(8,128)S(1)} all-to-all(f32[8,24,256]{2,1,0:T(8,128)S(1)} %bitcast.18), channel_id=1, replica_groups=mesh['x'=4,'y'=8,'core'=2,'col'=12] {'y'}, dimensions={0} | all-to-all | bytes 393216 | tf_op jit(solution)/shard_map/all_to_all | solution.py:44
  92.1 11.1 %all_to_all.38 = f32[8,24,256]{2,1,0:T(8,128)S(1)} all-to-all(f32[8,24,256]{2,1,0:T(8,128)S(1)} %add.16), channel_id=1, replica_groups=mesh['x'=4,'y'=8,'core'=2,'col'=12] {'y'}, dimensions={0} | all-to-all | bytes 393216 | tf_op jit(solution)/shard_map/all_to_all | solution.py:44
  103.2 0.1 broadcast_in_dim.3
  103.3 10.7 %all_to_all.39 = f32[4,192,256]{2,1,0:T(8,128)S(1)} all-to-all(f32[4,192,256]{2,1,0:T(8,128)S(1)} %broadcast_in_dim.3), channel_id=1, replica_groups=mesh['x'=4,'y'=8,'core'=2,'col'=12] {'x'}, dimensions={0} | all-to-all | bytes 1572864 | tf_op jit(solution)/shard_map/all_to_all | solution.py:44
  114.1 7.3 %collective-permute-start.2 = (f32[576,256]{1,0:T(8,128)S(1)}, f32[576,256]{1,0:T(8,128)S(1)}, u32[]{:S(2)}, u32[]{:S(2)}) collective-permute-start(f32[576,256]{1,0:T(8,128)S(1)} %bitcast.20), channel_id=1, source_target_pairs={{0,12},{12,0},{1,13},{13,1},{2,14},{14,2},{3,15},{15,3},{4,16},{16... | collective-permute-start | bytes 1769480 | tf_op jit(solution)/shard_map/ppermute | solution.py:324
  121.4 6.2 %inverse.1.inverse_ref = f32[256,256]{1,0:T(8,128)S(1)} custom-call(f32[768,256]{1,0:T(8,128)S(1)} %bitcast.12), custom_call_target="tpu_custom_call" | custom-call | flops 10000000000 | bytes 524288 | tf_op jit(solution)/shard_map/inverse/pallas_call | solution.py:325
  127.6 0.0 collective-permute-done.2.other_ref
  127.6 1.4 right.1
  129.0 3.5 %all-to-all-start.6 = ((f32[12,1,256]{2,1,0:T(1,128)}), f32[12,1,256]{2,1,0:T(1,128)S(1)}, u32[]{:S(2)}, u32[]{:S(2)}) async-start(f32[12,1,256]{2,1,0:T(1,128)} %get-tuple-element.16), calls=%async_computation.6 | async-start | bytes 24576 | tf_op jit(solution)/shard_map/all_to_all | solution.py:44
  132.5 2.4 %momentum.1 = f32[256,1152]{1,0:T(8,128)} custom-call(f32[256,1152]{1,0:T(8,128)S(1)} %copy-done, bf16[256,1152]{1,0:T(8,128)(2,1)S(1)} %copy-done.1, f32[256,256]{1,0:T(8,128)S(1)} %get-tuple-element.14.orthonormal_ref.left_ref, f32[1152,256]{1,0:T(8,128)S(1)} %get-tuple-element.15.right_ref), custom_call_target="tpu_custom_call" | custom-call | flops 1000000000 | bytes 4000000 | tf_op jit(solution)/shard_map/momentum/pallas_call | solution.py:262
  134.9 6.4 %all-to-all-done.6.squares_ref = f32[12,1,256]{2,1,0:T(1,128)S(1)} async-done(((f32[12,1,256]{2,1,0:T(1,128)}), f32[12,1,256]{2,1,0:T(1,128)S(1)}, u32[]{:S(2)}, u32[]{:S(2)}) %all-to-all-start.6) | async-done | bytes 12320 | tf_op jit(solution)/shard_map/all_to_all | solution.py:44
  141.4 1.6 %update.1 = (f32[1152,256]{1,0:T(8,128)}, bf16[256,1152]{1,0:T(8,128)(2,1)}) custom-call(f32[12,1,256]{2,1,0:T(1,128)S(1)} %all-to-all-done.6.squares_ref, f32[256,256]{1,0:T(8,128)S(1)} %get-tuple-element.14.orthonormal_ref.left_ref, f32[1152,256]{1,0:T(8,128)S(1)} %get-tuple-element.15.right_ref), custom_call_target="tpu_custom_call" | custom-call | flops 1000000000 | bytes 3000000 | tf_op jit(solution)/shard_map/update/pallas_call | solution.py:290
  (4 shorter events, 0.1 us)
Async XLA Ops:
  0.6 19.1 %copy-start = (f32[256,1152]{1,0:T(8,128)S(1)}, f32[256,1152]{1,0:T(8,128)}, u32[]{:S(2)}) copy-start(f32[256,1152]{1,0:T(8,128)} %momentum_ref.1) | copy-start | bytes 3538948
  4.0 30.9 %all-to-all-start = ((f32[12,24,256]{2,1,0:T(8,128)}), f32[12,24,256]{2,1,0:T(8,128)S(1)}, u32[]{:S(2)}, u32[]{:S(2)}) async-start(f32[12,24,256]{2,1,0:T(8,128)} %bitcast.21), calls=%async_computation | async-start | bytes 589824 | tf_op jit(solution)/shard_map/all_to_all | solution.py:44
  19.7 1.4 copy-start.1
  24.8 10.1 %collective-permute-start = (f32[256,576]{0,1:T(8,128)}, f32[256,576]{0,1:T(8,128)S(1)}, u32[]{:S(2)}, u32[]{:S(2)}) collective-permute-start(f32[256,576]{0,1:T(8,128)} %get-tuple-element.19), channel_id=1, source_target_pairs={{0,12},{12,0},{1,13},{13,1},{2,14},{14,2},{3,15},{15,3},{4,16},{16... | collective-permute-start | bytes 1769480 | tf_op jit(solution)/shard_map/ppermute | solution.py:312
  34.8 24.8 %copy-start.2 = (f32[576,256]{1,0:T(8,128)S(1)}, f32[576,256]{1,0:T(8,128)}, u32[]{:S(2)}) copy-start(f32[576,256]{1,0:T(8,128)} %get-tuple-element.11.blended_ref) | copy-start | bytes 1769476
  34.9 20.1 %copy-start.3 = (f32[256,576]{0,1:T(8,128)}, f32[256,576]{0,1:T(8,128)S(1)}, u32[]{:S(2)}) copy-start(f32[256,576]{0,1:T(8,128)S(1)} %collective-permute-done) | copy-start | bytes 1769476
  55.0 5.8 %collective-permute-start.1 = (f32[256,256]{1,0:T(8,128)S(1)}, f32[256,256]{1,0:T(8,128)S(1)}, u32[]{:S(2)}, u32[]{:S(2)}) collective-permute-start(f32[256,256]{1,0:T(8,128)S(1)} %slice.12), channel_id=1, source_target_pairs={{0,12},{12,0},{1,13},{13,1},{2,14},{14,2},{3,15},{15,3},{4,16},{16... | collective-permute-start | bytes 786440 | tf_op jit(solution)/shard_map/ppermute | solution.py:315
  59.7 1.1 copy-start.4
  114.1 13.5 %collective-permute-start.2 = (f32[576,256]{1,0:T(8,128)S(1)}, f32[576,256]{1,0:T(8,128)S(1)}, u32[]{:S(2)}, u32[]{:S(2)}) collective-permute-start(f32[576,256]{1,0:T(8,128)S(1)} %bitcast.20), channel_id=1, source_target_pairs={{0,12},{12,0},{1,13},{13,1},{2,14},{14,2},{3,15},{15,3},{4,16},{16... | collective-permute-start | bytes 1769480 | tf_op jit(solution)/shard_map/ppermute | solution.py:324
  129.0 12.4 %all-to-all-start.6 = ((f32[12,1,256]{2,1,0:T(1,128)}), f32[12,1,256]{2,1,0:T(1,128)S(1)}, u32[]{:S(2)}, u32[]{:S(2)}) async-start(f32[12,1,256]{2,1,0:T(1,128)} %get-tuple-element.16), calls=%async_computation.6 | async-start | bytes 24576 | tf_op jit(solution)/shard_map/all_to_all | solution.py:44

commit v4 on v3

--- a/solution.py
+++ b/solution.py
@@ -18,6 +18,7 @@
 epsilon = 1e-06
 
 ROW = ("x", "y", "core")
+COL = ("far", "near")
 SWAP = ((0, 1), (1, 0))
 HIGHEST = lax.Precision.HIGHEST
 
@@ -48,17 +49,16 @@
     return jnp.sum(exchange(parts, axes), axis=0)
 
 
-def all_sum(parts, axes, *ready):
+def add(parts, copies):
     def kernel(in_ref, out_ref):
         total = in_ref[0]
         for i in range(1, in_ref.shape[0]):
             total = total + in_ref[i]
-        for i in range(in_ref.shape[0]):
+        for i in range(copies):
             out_ref[i] = total
 
-    (sums,) = call(kernel, [parts.shape], (10_000_000, 2 * parts.size * 4), "add")(exchange(parts, axes))
-    sums, *ready = lax.optimization_barrier((sums, *ready))
-    return exchange(sums, axes), *ready
+    shape = (copies,) + parts.shape[1:]
+    return call(kernel, [shape], (10_000_000, 2 * parts.size * 4), "add")(parts)[0]
 
 
 def gather(part, axes, count):
@@ -179,7 +179,6 @@
         ])
         for copy in copies[k]:
             copy.start()
-    out_ref[256:288, :] = jnp.zeros((32, RANK), jnp.float32)
     total = None
     for k in range(3):
         for copy in copies[k]:
@@ -187,7 +186,7 @@
         blended = momentum_ref[k] + gradient_ref[k].astype(jnp.float32)
         part = product(blended, factor_ref[k], ((1,), (0,)))
         total = part if total is None else total + part
-    out_ref[0:256, :] = total
+    out_ref[...] = total
 
 
 def left(momentum, gradient, right_factor, product=dot3):
@@ -196,7 +195,7 @@
         functools.partial(left_kernel, product),
         in_specs=[hbm] * 3,
         out_specs=pl.BlockSpec(memory_space=pltpu.VMEM),
-        out_shape=jax.ShapeDtypeStruct((288, RANK), jnp.float32),
+        out_shape=jax.ShapeDtypeStruct((256, RANK), jnp.float32),
         scratch_shapes=[
             pltpu.VMEM((3, 256, STEP), jnp.float32),
             pltpu.VMEM((3, 256, STEP), jnp.bfloat16),
@@ -215,7 +214,7 @@
 
 
 def own_sums_kernel(blended_ref, left_ref, out_ref):
-    left = left_ref[0:256, :]
+    left = left_ref[...]
     out_ref[0:576, :] = dot3(blended_ref[...], left, ((1,), (0,)))
     out_ref[576:768, :] = fold_gram(dot(left, left, ((0,), (0,))))
 
@@ -236,7 +235,7 @@
     squares_ref[...] = jnp.broadcast_to(squares.reshape(1, 1, RANK), (12, 1, RANK))
     copy = pltpu.make_async_copy(squares_ref, squares_hbm, sem)
     copy.start()
-    orthonormal_ref[...] = dot3(left_ref[0:256, :], inverse, ((1,), (1,)))
+    orthonormal_ref[...] = dot3(left_ref[...], inverse, ((1,), (1,)))
 
     @pl.when(core_ref[0] == 0)
     def _():
@@ -307,18 +306,20 @@
     core = lax.axis_index("core")
     left_parts = left(momentum, gradient, right_factor)
     blended = momentum + gradient.astype(jnp.float32)
+    sums = add(exchange(left_parts.reshape(4, 64, RANK), "near"), 3)
+    sums, blended = lax.optimization_barrier((sums, blended))
     kept = lax.dynamic_slice(blended, (0, core * 576), (256, 576))
     sent = lax.dynamic_slice(blended, (0, (1 - core) * 576), (256, 576))
     taken = lax.ppermute(sent, "core", SWAP)
-    left_own, kept, taken = all_sum(left_parts.reshape(12, 24, RANK), "col", kept.T, taken.T)
-    left_own = left_own.reshape(288, RANK)
-    left_other = lax.ppermute(left_own[:256], "core", SWAP)
+    sums = add(exchange(sums, "far"), 4)
+    sums, kept, taken = lax.optimization_barrier((sums, kept.T, taken.T))
+    left_own = exchange(sums, "near").reshape(256, RANK)
+    left_other = lax.ppermute(left_own, "core", SWAP)
     cost = (500_000_000, 3_000_000)
     (own,) = call(own_sums_kernel, [(768, RANK)], cost, "own_sums")(kept, left_own)
     (sums,) = call(other_sums_kernel, [(768, RANK)], cost, "other_sums")(own, taken, left_other)
     part = scatter_sum(sums.reshape(4, 192, RANK), "x")
-    (part,) = all_sum(part.reshape(8, 24, RANK), "y")
-    part = part.reshape(192, RANK)
+    part = exchange(add(exchange(part.reshape(8, 24, RANK), "y"), 8), "y").reshape(192, RANK)
     part = gather(part, "x", 4).reshape(768, RANK)
 
     right_theirs = lax.ppermute(part[:576], "core", SWAP)
@@ -330,18 +331,18 @@
         out_specs=[vmem, vmem, pl.BlockSpec(memory_space=pl.ANY)],
         scratch_shapes=[pltpu.VMEM((12, 1, RANK), jnp.float32), pltpu.SemaphoreType.DMA],
     )(core.reshape(1), inverse, left_own, part, right_theirs)
-    squares = exchange(squares, "col")
+    squares = exchange(squares, COL)
     (new_momentum,) = feedback(momentum, gradient, orthonormal, right_full)
     new_right, update = last(squares, orthonormal, right_full)
     return (new_momentum, new_right, update)
 
 
 def solution(mesh):
-    fine = Mesh(mesh.devices.reshape(4, 8, 2, 12), ("x", "y", "core", "col"))
+    fine = Mesh(mesh.devices.reshape(4, 8, 2, 3, 4), ROW + COL)
     return jax.shard_map(
         on_device,
         mesh=fine,
-        in_specs=(P(ROW, "col"), P(ROW, "col"), P("col", None)),
-        out_specs=(P(ROW, "col"), P("col", None), P(ROW, "col")),
+        in_specs=(P(ROW, COL), P(ROW, COL), P(COL, None)),
+        out_specs=(P(ROW, COL), P(COL, None), P(ROW, COL)),
         check_vma=False,
     )

time: 144 us -> 145 us (level)
  blocking collectives: 72.5 us -> 81.4 us
  waiting for transfers between devices: 14.1 us -> 8.67 us
    all_to_all x5 -> x6, blocking collectives: 72.5 us -> 81.4 us  [exchange(): return lax.all_to_all(parts, axes, 0, 0, tiled=True)]
    all_to_all x2, starting transfers between devices: 19.2 us -> 12.3 us  [exchange(): return lax.all_to_all(parts, axes, 0, 0, tiled=True)]
    ppermute x1, starting transfers between devices: 2.85 us -> 9.14 us  [on_device(): taken = lax.ppermute(sent, 'core', SWAP)]
    all_to_all x2, waiting for transfers between devices: 13.6 us -> 8.17 us  [exchange(): return lax.all_to_all(parts, axes, 0, 0, tiled=True)]
  transfers between devices with their start and end apart: 5 -> 5, of which waited for: 3 -> 3; matrix products, arithmetic and copies ran while one was open for 4% -> 3% of each run, Pallas kernels for 7% -> 6%
where the time goes in v4:
time: 145 us; the launch traced here: 144 us
  blocking collectives  81.4 us (56%)
  starting transfers between devices  33.2 us (23%)
  Pallas kernels  16.3 us (11%)
  waiting for transfers between devices  8.67 us (6%)
  local copies, waits for them, and re-layouts  2.63 us (2%)
  other arithmetic  1.59 us (1%)
    all_to_all x6, blocking collectives, exchange(): return lax.all_to_all(parts, axes, 0, 0, tiled=True)  81.4 us
    all_to_all x2, starting transfers between devices, exchange(): return lax.all_to_all(parts, axes, 0, 0, tiled=True)  12.3 us
    ppermute x1, starting transfers between devices, on_device(): taken = lax.ppermute(sent, 'core', SWAP)  9.14 us
    all_to_all x2, waiting for transfers between devices, exchange(): return lax.all_to_all(parts, axes, 0, 0, tiled=True)  8.17 us
    ppermute x1, starting transfers between devices, on_device(): right_theirs = lax.ppermute(part[:576], 'core', SWAP)  7.31 us
    pallas_call x1, Pallas kernels, on_device(): call(invert_factor_kernel, [(RANK, RANK)], (10000000000, 524288), 'inverse')  6.21 us
    ppermute x1, starting transfers between devices, on_device(): left_other = lax.ppermute(left_own, 'core', SWAP)  4.52 us
    pallas_call x1, Pallas kernels, left(): pl.pallas_call(functools.partial(left_kernel, product), in_specs=[hbm] *...  3.31 us
  transfers between devices with their start and end apart: 5, of which 3 were waited for; matrix products, arithmetic and copies ran while one was open for 3% of the time, Pallas kernels for 6%

profile of v4, /device:TPU:1, one launch (start us, length us, event | category | flops | bytes accessed | tf_op | source)
XLA Modules:
  0.0 144.5 jit_solution(10077071195060109966)
XLA Ops:
  0.6 0.0 copy-start
  0.6 3.3 %left.1 = f32[256,256]{1,0:T(8,128)} custom-call(f32[256,1152]{1,0:T(8,128)} %momentum_ref.1, bf16[256,1152]{1,0:T(8,128)(2,1)} %gradient_ref.1, f32[1152,256]{1,0:T(8,128)} %factor_hbm.1), custom_call_target="tpu_custom_call" | custom-call | flops 1000000000 | bytes 3000000 | tf_op jit(solution)/shard_map/left/pallas_call | solution.py:194
  4.0 7.8 %all-to-all-start = ((f32[4,64,256]{2,1,0:T(8,128)}), f32[4,64,256]{2,1,0:T(8,128)S(1)}, u32[]{:S(2)}, u32[]{:S(2)}) async-start(f32[4,64,256]{2,1,0:T(8,128)} %bitcast.21), calls=%async_computation | async-start | bytes 524288 | tf_op jit(solution)/shard_map/all_to_all | solution.py:45
  11.8 0.0 copy-done
  11.8 0.0 copy-start.1
  11.8 1.4 copy.7
  13.2 0.0 copy-done.1
  13.2 1.1 copy.6
  14.2 1.5 %convert_add_fusion = f32[256,1152]{0,1:T(8,128)S(1)} fusion(f32[256,1152]{0,1:T(8,128)} %copy.7, bf16[256,1152]{0,1:T(8,128)(2,1)} %copy.6), kind=kLoop, calls=%fused_computation | loop fusion | flops 589824 | bytes 2949120 | tf_op jit(solution)/shard_map/add | solution.py:308
  15.8 1.6 %all-to-all-done.in_ref = f32[4,64,256]{2,1,0:T(8,128)S(1)} async-done(((f32[4,64,256]{2,1,0:T(8,128)}), f32[4,64,256]{2,1,0:T(8,128)S(1)}, u32[]{:S(2)}, u32[]{:S(2)}) %all-to-all-start) | async-done | bytes 262176 | tf_op jit(solution)/shard_map/all_to_all | solution.py:45
  17.4 0.1 constant_dynamic-slice_fusion
  17.5 9.1 %collective-permute-start = (f32[256,576]{0,1:T(8,128)S(1)}, f32[256,576]{0,1:T(8,128)S(1)}, u32[]{:S(2)}, u32[]{:S(2)}) collective-permute-start(f32[256,576]{0,1:T(8,128)S(1)} %get-tuple-element.23), channel_id=1, source_target_pairs={{0,12},{12,0},{1,13},{13,1},{2,14},{14,2},{3,15},{15,3},{4,16},{16... | collective-permute-start | bytes 1769480 | tf_op jit(solution)/shard_map/ppermute | solution.py:313
  26.7 19.4 %all_to_all.40.in_ref = f32[3,64,256]{2,1,0:T(8,128)S(1)} all-to-all(f32[3,64,256]{2,1,0:T(8,128)S(1)} %add.16), channel_id=1, replica_groups=mesh['x'=4,'y'=8,'core'=2,'far'=3,'near'=4] {'far'}, dimensions={0} | all-to-all | bytes 393216 | tf_op jit(solution)/shard_map/all_to_all | solution.py:45
  46.1 0.0 collective-permute-done
  46.1 9.6 %all_to_all.41 = f32[4,64,256]{2,1,0:T(8,128)S(1)} all-to-all(f32[4,64,256]{2,1,0:T(8,128)S(1)} %add.17), channel_id=1, replica_groups=mesh['x'=4,'y'=8,'core'=2,'far'=3,'near'=4] {'near'}, dimensions={0} | all-to-all | bytes 524288 | tf_op jit(solution)/shard_map/all_to_all | solution.py:45
  55.7 4.5 %collective-permute-start.1 = (f32[256,256]{1,0:T(8,128)S(1)}, f32[256,256]{1,0:T(8,128)S(1)}, u32[]{:S(2)}, u32[]{:S(2)}) collective-permute-start(f32[256,256]{1,0:T(8,128)S(1)} %bitcast.15), channel_id=1, source_target_pairs={{0,12},{12,0},{1,13},{13,1},{2,14},{14,2},{3,15},{15,3},{4,16},{16... | collective-permute-start | bytes 786440 | tf_op jit(solution)/shard_map/ppermute | solution.py:317
  60.2 0.6 own_sums.1.own_ref
  60.8 0.5 collective-permute-done.1.left_ref
  61.3 0.6 other_sums.1
  62.0 15.2 %all_to_all.42 = f32[4,192,256]{2,1,0:T(8,128)S(1)} all-to-all(f32[4,192,256]{2,1,0:T(8,128)S(1)} %bitcast.11), channel_id=1, replica_groups=mesh['x'=4,'y'=8,'core'=2,'far'=3,'near'=4] {'x'}, dimensions={0} | all-to-all | bytes 1572864 | tf_op jit(solution)/shard_map/all_to_all | solution.py:45
  77.2 0.1 reduce_sum.9
  77.3 15.3 %all_to_all.43.in_ref = f32[8,24,256]{2,1,0:T(8,128)S(1)} all-to-all(f32[8,24,256]{2,1,0:T(8,128)S(1)} %bitcast.18), channel_id=1, replica_groups=mesh['x'=4,'y'=8,'core'=2,'far'=3,'near'=4] {'y'}, dimensions={0} | all-to-all | bytes 393216 | tf_op jit(solution)/shard_map/all_to_all | solution.py:45
  92.6 11.1 %all_to_all.44 = f32[8,24,256]{2,1,0:T(8,128)S(1)} all-to-all(f32[8,24,256]{2,1,0:T(8,128)S(1)} %add.18), channel_id=1, replica_groups=mesh['x'=4,'y'=8,'core'=2,'far'=3,'near'=4] {'y'}, dimensions={0} | all-to-all | bytes 393216 | tf_op jit(solution)/shard_map/all_to_all | solution.py:45
  103.7 0.1 broadcast_in_dim.3
  103.8 10.7 %all_to_all.45 = f32[4,192,256]{2,1,0:T(8,128)S(1)} all-to-all(f32[4,192,256]{2,1,0:T(8,128)S(1)} %broadcast_in_dim.3), channel_id=1, replica_groups=mesh['x'=4,'y'=8,'core'=2,'far'=3,'near'=4] {'x'}, dimensions={0} | all-to-all | bytes 1572864 | tf_op jit(solution)/shard_map/all_to_all | solution.py:45
  114.6 7.3 %collective-permute-start.2 = (f32[576,256]{1,0:T(8,128)S(1)}, f32[576,256]{1,0:T(8,128)S(1)}, u32[]{:S(2)}, u32[]{:S(2)}) collective-permute-start(f32[576,256]{1,0:T(8,128)S(1)} %bitcast.20), channel_id=1, source_target_pairs={{0,12},{12,0},{1,13},{13,1},{2,14},{14,2},{3,15},{15,3},{4,16},{16... | collective-permute-start | bytes 1769480 | tf_op jit(solution)/shard_map/ppermute | solution.py:325
  121.9 6.2 %inverse.1.inverse_ref = f32[256,256]{1,0:T(8,128)S(1)} custom-call(f32[768,256]{1,0:T(8,128)S(1)} %bitcast.12), custom_call_target="tpu_custom_call" | custom-call | flops 10000000000 | bytes 524288 | tf_op jit(solution)/shard_map/inverse/pallas_call | solution.py:326
  128.1 0.0 collective-permute-done.2.other_ref
  128.1 1.4 right.1
  129.5 4.4 %all-to-all-start.7 = ((f32[12,1,256]{2,1,0:T(1,128)}), f32[12,1,256]{2,1,0:T(1,128)S(1)}, u32[]{:S(2)}, u32[]{:S(2)}) async-start(f32[12,1,256]{2,1,0:T(1,128)} %get-tuple-element.20), calls=%async_computation.7 | async-start | bytes 24576 | tf_op jit(solution)/shard_map/all_to_all | solution.py:45
  133.9 2.4 %momentum.1 = f32[256,1152]{1,0:T(8,128)} custom-call(f32[256,1152]{1,0:T(8,128)S(1)} %copy-done, bf16[256,1152]{1,0:T(8,128)(2,1)S(1)} %copy-done.1, f32[256,256]{1,0:T(8,128)S(1)} %get-tuple-element.18.orthonormal_ref.left_ref, f32[1152,256]{1,0:T(8,128)S(1)} %get-tuple-element.19.right_ref), custom_call_target="tpu_custom_call" | custom-call | flops 1000000000 | bytes 4000000 | tf_op jit(solution)/shard_map/momentum/pallas_call | solution.py:261
  136.4 6.5 %all-to-all-done.7.squares_ref = f32[12,1,256]{2,1,0:T(1,128)S(1)} async-done(((f32[12,1,256]{2,1,0:T(1,128)}), f32[12,1,256]{2,1,0:T(1,128)S(1)}, u32[]{:S(2)}, u32[]{:S(2)}) %all-to-all-start.7) | async-done | bytes 12320 | tf_op jit(solution)/shard_map/all_to_all | solution.py:45
  142.9 1.6 %update.1 = (f32[1152,256]{1,0:T(8,128)}, bf16[256,1152]{1,0:T(8,128)(2,1)}) custom-call(f32[12,1,256]{2,1,0:T(1,128)S(1)} %all-to-all-done.7.squares_ref, f32[256,256]{1,0:T(8,128)S(1)} %get-tuple-element.18.orthonormal_ref.left_ref, f32[1152,256]{1,0:T(8,128)S(1)} %get-tuple-element.19.right_ref), custom_call_target="tpu_custom_call" | custom-call | flops 1000000000 | bytes 3000000 | tf_op jit(solution)/shard_map/update/pallas_call | solution.py:289
  (4 shorter events, 0.1 us)
Async XLA Ops:
  0.6 11.1 %copy-start = (f32[256,1152]{1,0:T(8,128)S(1)}, f32[256,1152]{1,0:T(8,128)}, u32[]{:S(2)}) copy-start(f32[256,1152]{1,0:T(8,128)} %momentum_ref.1) | copy-start | bytes 3538948
  4.0 13.4 %all-to-all-start = ((f32[4,64,256]{2,1,0:T(8,128)}), f32[4,64,256]{2,1,0:T(8,128)S(1)}, u32[]{:S(2)}, u32[]{:S(2)}) async-start(f32[4,64,256]{2,1,0:T(8,128)} %bitcast.21), calls=%async_computation | async-start | bytes 524288 | tf_op jit(solution)/shard_map/all_to_all | solution.py:45
  11.8 1.4 copy-start.1
  17.5 28.5 %collective-permute-start = (f32[256,576]{0,1:T(8,128)S(1)}, f32[256,576]{0,1:T(8,128)S(1)}, u32[]{:S(2)}, u32[]{:S(2)}) collective-permute-start(f32[256,576]{0,1:T(8,128)S(1)} %get-tuple-element.23), channel_id=1, source_target_pairs={{0,12},{12,0},{1,13},{13,1},{2,14},{14,2},{3,15},{15,3},{4,16},{16... | collective-permute-start | bytes 1769480 | tf_op jit(solution)/shard_map/ppermute | solution.py:313
  55.7 5.7 %collective-permute-start.1 = (f32[256,256]{1,0:T(8,128)S(1)}, f32[256,256]{1,0:T(8,128)S(1)}, u32[]{:S(2)}, u32[]{:S(2)}) collective-permute-start(f32[256,256]{1,0:T(8,128)S(1)} %bitcast.15), channel_id=1, source_target_pairs={{0,12},{12,0},{1,13},{13,1},{2,14},{14,2},{3,15},{15,3},{4,16},{16... | collective-permute-start | bytes 786440 | tf_op jit(solution)/shard_map/ppermute | solution.py:317
  114.6 13.5 %collective-permute-start.2 = (f32[576,256]{1,0:T(8,128)S(1)}, f32[576,256]{1,0:T(8,128)S(1)}, u32[]{:S(2)}, u32[]{:S(2)}) collective-permute-start(f32[576,256]{1,0:T(8,128)S(1)} %bitcast.20), channel_id=1, source_target_pairs={{0,12},{12,0},{1,13},{13,1},{2,14},{14,2},{3,15},{15,3},{4,16},{16... | collective-permute-start | bytes 1769480 | tf_op jit(solution)/shard_map/ppermute | solution.py:325
  129.5 13.4 %all-to-all-start.7 = ((f32[12,1,256]{2,1,0:T(1,128)}), f32[12,1,256]{2,1,0:T(1,128)S(1)}, u32[]{:S(2)}, u32[]{:S(2)}) async-start(f32[12,1,256]{2,1,0:T(1,128)} %get-tuple-element.20), calls=%async_computation.7 | async-start | bytes 24576 | tf_op jit(solution)/shard_map/all_to_all | solution.py:45

commit v5 on v3

--- a/solution.py
+++ b/solution.py
@@ -166,26 +166,28 @@
 
 
 STEP = 384
+PIECES = ((0, 512), (512, 384), (896, 256))
 
 
 def left_kernel(product, momentum_hbm, gradient_hbm, factor_hbm, out_ref, momentum_ref, gradient_ref, factor_ref, sems):
     copies = []
-    for k in range(3):
-        at = pl.ds(k * STEP, STEP)
+    for k, (start, size) in enumerate(PIECES):
+        at = pl.ds(start, size)
         copies.append([
-            pltpu.make_async_copy(momentum_hbm.at[:, at], momentum_ref.at[k], sems.at[k, 0]),
-            pltpu.make_async_copy(factor_hbm.at[at, :], factor_ref.at[k], sems.at[k, 1]),
-            pltpu.make_async_copy(gradient_hbm.at[:, at], gradient_ref.at[k], sems.at[k, 2]),
+            pltpu.make_async_copy(momentum_hbm.at[:, at], momentum_ref.at[:, at], sems.at[k, 0]),
+            pltpu.make_async_copy(factor_hbm.at[at, :], factor_ref.at[at, :], sems.at[k, 1]),
+            pltpu.make_async_copy(gradient_hbm.at[:, at], gradient_ref.at[:, at], sems.at[k, 2]),
         ])
         for copy in copies[k]:
             copy.start()
     out_ref[256:288, :] = jnp.zeros((32, RANK), jnp.float32)
     total = None
-    for k in range(3):
+    for k, (start, size) in enumerate(PIECES):
         for copy in copies[k]:
             copy.wait()
-        blended = momentum_ref[k] + gradient_ref[k].astype(jnp.float32)
-        part = product(blended, factor_ref[k], ((1,), (0,)))
+        at = pl.ds(start, size)
+        blended = momentum_ref[:, at] + gradient_ref[:, at].astype(jnp.float32)
+        part = product(blended, factor_ref[at, :], ((1,), (0,)))
         total = part if total is None else total + part
     out_ref[0:256, :] = total
 
@@ -198,9 +200,9 @@
         out_specs=pl.BlockSpec(memory_space=pltpu.VMEM),
         out_shape=jax.ShapeDtypeStruct((288, RANK), jnp.float32),
         scratch_shapes=[
-            pltpu.VMEM((3, 256, STEP), jnp.float32),
-            pltpu.VMEM((3, 256, STEP), jnp.bfloat16),
-            pltpu.VMEM((3, STEP, RANK), jnp.float32),
+            pltpu.VMEM((256, 1152), jnp.float32),
+            pltpu.VMEM((256, 1152), jnp.bfloat16),
+            pltpu.VMEM((1152, RANK), jnp.float32),
             pltpu.SemaphoreType.DMA((3, 3)),
         ],
         compiler_params=pltpu.CompilerParams(vmem_limit_bytes=60 << 20),

time: 144 us -> 144 us (level)
  no operation moved by 1% of the time
where the time goes in v5:
time: 144 us; the launch traced here: 143 us
  blocking collectives  72.5 us (50%)
  starting transfers between devices  34 us (24%)
  Pallas kernels  16.2 us (11%)
  waiting for transfers between devices  14.1 us (10%)
  local copies, waits for them, and re-layouts  3.68 us (3%)
  other arithmetic  1.59 us (1%)
    all_to_all x5, blocking collectives, exchange(): return lax.all_to_all(parts, axes, 0, 0, tiled=True)  72.5 us
    all_to_all x2, starting transfers between devices, exchange(): return lax.all_to_all(parts, axes, 0, 0, tiled=True)  19.2 us
    all_to_all x2, waiting for transfers between devices, exchange(): return lax.all_to_all(parts, axes, 0, 0, tiled=True)  13.6 us
    ppermute x1, starting transfers between devices, on_device(): right_theirs = lax.ppermute(part[:576], 'core', SWAP)  7.31 us
    pallas_call x1, Pallas kernels, on_device(): call(invert_factor_kernel, [(RANK, RANK)], (10000000000, 524288), 'inverse')  6.21 us
    ppermute x1, starting transfers between devices, on_device(): left_other = lax.ppermute(left_own[:256], 'core', SWAP)  4.65 us
    pallas_call x1, Pallas kernels, left(): pl.pallas_call(functools.partial(left_kernel, product), in_specs=[hbm] *...  3.29 us
  transfers between devices with their start and end apart: 5, of which 3 were waited for; matrix products, arithmetic and copies ran while one was open for 4% of the time, Pallas kernels for 7%

profile of v5, /device:TPU:1, one launch (start us, length us, event | category | flops | bytes accessed | tf_op | source)
XLA Modules:
  0.0 142.9 jit_solution(977525318046856610)
XLA Ops:
  0.6 0.0 copy-start
  0.6 3.3 %left.1 = f32[288,256]{1,0:T(8,128)} custom-call(f32[256,1152]{1,0:T(8,128)} %momentum_ref.1, bf16[256,1152]{1,0:T(8,128)(2,1)} %gradient_ref.1, f32[1152,256]{1,0:T(8,128)} %factor_hbm.1), custom_call_target="tpu_custom_call" | custom-call | flops 1000000000 | bytes 3000000 | tf_op jit(solution)/shard_map/left/pallas_call | solution.py:197
  3.9 15.7 %all-to-all-start = ((f32[12,24,256]{2,1,0:T(8,128)}), f32[12,24,256]{2,1,0:T(8,128)S(1)}, u32[]{:S(2)}, u32[]{:S(2)}) async-start(f32[12,24,256]{2,1,0:T(8,128)} %bitcast.21), calls=%async_computation | async-start | bytes 589824 | tf_op jit(solution)/shard_map/all_to_all | solution.py:44
  19.7 0.0 copy-done
  19.7 0.0 copy-start.1
  19.7 1.4 copy.7
  21.1 0.0 copy-done.1
  21.1 1.1 copy.6
  22.1 1.5 %convert_add_fusion = f32[256,1152]{0,1:T(8,128)S(1)} fusion(f32[256,1152]{0,1:T(8,128)} %copy.7, bf16[256,1152]{0,1:T(8,128)(2,1)} %copy.6), kind=kLoop, calls=%fused_computation | loop fusion | flops 589824 | bytes 2949120 | tf_op jit(solution)/shard_map/add | solution.py:311
  23.7 1.1 constant_dynamic-slice_fusion
  24.8 2.9 %collective-permute-start = (f32[256,576]{0,1:T(8,128)}, f32[256,576]{0,1:T(8,128)S(1)}, u32[]{:S(2)}, u32[]{:S(2)}) collective-permute-start(f32[256,576]{0,1:T(8,128)} %get-tuple-element.19), channel_id=1, source_target_pairs={{0,12},{12,0},{1,13},{13,1},{2,14},{14,2},{3,15},{15,3},{4,16},{16... | collective-permute-start | bytes 1769480 | tf_op jit(solution)/shard_map/ppermute | solution.py:314
  27.6 7.2 %all-to-all-done.in_ref = f32[12,24,256]{2,1,0:T(8,128)S(1)} async-done(((f32[12,24,256]{2,1,0:T(8,128)}), f32[12,24,256]{2,1,0:T(8,128)S(1)}, u32[]{:S(2)}, u32[]{:S(2)}) %all-to-all-start) | async-done | bytes 294944 | tf_op jit(solution)/shard_map/all_to_all | solution.py:44
  34.8 0.0 copy-start.2
  34.9 0.0 collective-permute-done
  34.9 0.0 copy-start.3
  34.9 20.1 %all_to_all.35 = f32[12,24,256]{2,1,0:T(8,128)S(1)} all-to-all(f32[12,24,256]{2,1,0:T(8,128)S(1)} %add.15), channel_id=1, replica_groups=mesh['x'=4,'y'=8,'core'=2,'col'=12] {'col'}, dimensions={0} | all-to-all | bytes 589824 | tf_op jit(solution)/shard_map/all_to_all | solution.py:44
  55.0 0.0 copy-done.3
  55.0 4.7 %collective-permute-start.1 = (f32[256,256]{1,0:T(8,128)S(1)}, f32[256,256]{1,0:T(8,128)S(1)}, u32[]{:S(2)}, u32[]{:S(2)}) collective-permute-start(f32[256,256]{1,0:T(8,128)S(1)} %slice.12), channel_id=1, source_target_pairs={{0,12},{12,0},{1,13},{13,1},{2,14},{14,2},{3,15},{15,3},{4,16},{16... | collective-permute-start | bytes 786440 | tf_op jit(solution)/shard_map/ppermute | solution.py:317
  59.7 0.0 copy-done.2
  59.7 0.0 copy-start.4
  59.7 0.6 own_sums.1.own_ref
  60.3 0.5 collective-permute-done.1.left_ref
  60.8 0.0 copy-done.4
  60.8 0.6 other_sums.1
  61.5 15.2 %all_to_all.36 = f32[4,192,256]{2,1,0:T(8,128)S(1)} all-to-all(f32[4,192,256]{2,1,0:T(8,128)S(1)} %bitcast.11), channel_id=1, replica_groups=mesh['x'=4,'y'=8,'core'=2,'col'=12] {'x'}, dimensions={0} | all-to-all | bytes 1572864 | tf_op jit(solution)/shard_map/all_to_all | solution.py:44
  76.7 0.1 reduce_sum.9
  76.7 15.3 %all_to_all.37.in_ref = f32[8,24,256]{2,1,0:T(8,128)S(1)} all-to-all(f32[8,24,256]{2,1,0:T(8,128)S(1)} %bitcast.18), channel_id=1, replica_groups=mesh['x'=4,'y'=8,'core'=2,'col'=12] {'y'}, dimensions={0} | all-to-all | bytes 393216 | tf_op jit(solution)/shard_map/all_to_all | solution.py:44
  92.1 11.1 %all_to_all.38 = f32[8,24,256]{2,1,0:T(8,128)S(1)} all-to-all(f32[8,24,256]{2,1,0:T(8,128)S(1)} %add.16), channel_id=1, replica_groups=mesh['x'=4,'y'=8,'core'=2,'col'=12] {'y'}, dimensions={0} | all-to-all | bytes 393216 | tf_op jit(solution)/shard_map/all_to_all | solution.py:44
  103.2 0.1 broadcast_in_dim.3
  103.3 10.7 %all_to_all.39 = f32[4,192,256]{2,1,0:T(8,128)S(1)} all-to-all(f32[4,192,256]{2,1,0:T(8,128)S(1)} %broadcast_in_dim.3), channel_id=1, replica_groups=mesh['x'=4,'y'=8,'core'=2,'col'=12] {'x'}, dimensions={0} | all-to-all | bytes 1572864 | tf_op jit(solution)/shard_map/all_to_all | solution.py:44
  114.0 7.3 %collective-permute-start.2 = (f32[576,256]{1,0:T(8,128)S(1)}, f32[576,256]{1,0:T(8,128)S(1)}, u32[]{:S(2)}, u32[]{:S(2)}) collective-permute-start(f32[576,256]{1,0:T(8,128)S(1)} %bitcast.20), channel_id=1, source_target_pairs={{0,12},{12,0},{1,13},{13,1},{2,14},{14,2},{3,15},{15,3},{4,16},{16... | collective-permute-start | bytes 1769480 | tf_op jit(solution)/shard_map/ppermute | solution.py:326
  121.4 6.2 %inverse.1.inverse_ref = f32[256,256]{1,0:T(8,128)S(1)} custom-call(f32[768,256]{1,0:T(8,128)S(1)} %bitcast.12), custom_call_target="tpu_custom_call" | custom-call | flops 10000000000 | bytes 524288 | tf_op jit(solution)/shard_map/inverse/pallas_call | solution.py:327
  127.6 0.0 collective-permute-done.2.other_ref
  127.6 1.4 right.1
  129.0 3.5 %all-to-all-start.6 = ((f32[12,1,256]{2,1,0:T(1,128)}), f32[12,1,256]{2,1,0:T(1,128)S(1)}, u32[]{:S(2)}, u32[]{:S(2)}) async-start(f32[12,1,256]{2,1,0:T(1,128)} %get-tuple-element.16), calls=%async_computation.6 | async-start | bytes 24576 | tf_op jit(solution)/shard_map/all_to_all | solution.py:44
  132.5 2.4 %momentum.1 = f32[256,1152]{1,0:T(8,128)} custom-call(f32[256,1152]{1,0:T(8,128)S(1)} %copy-done, bf16[256,1152]{1,0:T(8,128)(2,1)S(1)} %copy-done.1, f32[256,256]{1,0:T(8,128)S(1)} %get-tuple-element.14.orthonormal_ref.left_ref, f32[1152,256]{1,0:T(8,128)S(1)} %get-tuple-element.15.right_ref), custom_call_target="tpu_custom_call" | custom-call | flops 1000000000 | bytes 4000000 | tf_op jit(solution)/shard_map/momentum/pallas_call | solution.py:264
  134.9 6.4 %all-to-all-done.6.squares_ref = f32[12,1,256]{2,1,0:T(1,128)S(1)} async-done(((f32[12,1,256]{2,1,0:T(1,128)}), f32[12,1,256]{2,1,0:T(1,128)S(1)}, u32[]{:S(2)}, u32[]{:S(2)}) %all-to-all-start.6) | async-done | bytes 12320 | tf_op jit(solution)/shard_map/all_to_all | solution.py:44
  141.4 1.6 %update.1 = (f32[1152,256]{1,0:T(8,128)}, bf16[256,1152]{1,0:T(8,128)(2,1)}) custom-call(f32[12,1,256]{2,1,0:T(1,128)S(1)} %all-to-all-done.6.squares_ref, f32[256,256]{1,0:T(8,128)S(1)} %get-tuple-element.14.orthonormal_ref.left_ref, f32[1152,256]{1,0:T(8,128)S(1)} %get-tuple-element.15.right_ref), custom_call_target="tpu_custom_call" | custom-call | flops 1000000000 | bytes 3000000 | tf_op jit(solution)/shard_map/update/pallas_call | solution.py:292
  (4 shorter events, 0.1 us)
Async XLA Ops:
  0.6 19.0 %copy-start = (f32[256,1152]{1,0:T(8,128)S(1)}, f32[256,1152]{1,0:T(8,128)}, u32[]{:S(2)}) copy-start(f32[256,1152]{1,0:T(8,128)} %momentum_ref.1) | copy-start | bytes 3538948
  3.9 30.9 %all-to-all-start = ((f32[12,24,256]{2,1,0:T(8,128)}), f32[12,24,256]{2,1,0:T(8,128)S(1)}, u32[]{:S(2)}, u32[]{:S(2)}) async-start(f32[12,24,256]{2,1,0:T(8,128)} %bitcast.21), calls=%async_computation | async-start | bytes 589824 | tf_op jit(solution)/shard_map/all_to_all | solution.py:44
  19.7 1.4 copy-start.1
  24.8 10.1 %collective-permute-start = (f32[256,576]{0,1:T(8,128)}, f32[256,576]{0,1:T(8,128)S(1)}, u32[]{:S(2)}, u32[]{:S(2)}) collective-permute-start(f32[256,576]{0,1:T(8,128)} %get-tuple-element.19), channel_id=1, source_target_pairs={{0,12},{12,0},{1,13},{13,1},{2,14},{14,2},{3,15},{15,3},{4,16},{16... | collective-permute-start | bytes 1769480 | tf_op jit(solution)/shard_map/ppermute | solution.py:314
  34.8 24.8 %copy-start.2 = (f32[576,256]{1,0:T(8,128)S(1)}, f32[576,256]{1,0:T(8,128)}, u32[]{:S(2)}) copy-start(f32[576,256]{1,0:T(8,128)} %get-tuple-element.11.blended_ref) | copy-start | bytes 1769476
  34.9 20.1 %copy-start.3 = (f32[256,576]{0,1:T(8,128)}, f32[256,576]{0,1:T(8,128)S(1)}, u32[]{:S(2)}) copy-start(f32[256,576]{0,1:T(8,128)S(1)} %collective-permute-done) | copy-start | bytes 1769476
  55.0 5.8 %collective-permute-start.1 = (f32[256,256]{1,0:T(8,128)S(1)}, f32[256,256]{1,0:T(8,128)S(1)}, u32[]{:S(2)}, u32[]{:S(2)}) collective-permute-start(f32[256,256]{1,0:T(8,128)S(1)} %slice.12), channel_id=1, source_target_pairs={{0,12},{12,0},{1,13},{13,1},{2,14},{14,2},{3,15},{15,3},{4,16},{16... | collective-permute-start | bytes 786440 | tf_op jit(solution)/shard_map/ppermute | solution.py:317
  59.7 1.1 copy-start.4
  114.0 13.5 %collective-permute-start.2 = (f32[576,256]{1,0:T(8,128)S(1)}, f32[576,256]{1,0:T(8,128)S(1)}, u32[]{:S(2)}, u32[]{:S(2)}) collective-permute-start(f32[576,256]{1,0:T(8,128)S(1)} %bitcast.20), channel_id=1, source_target_pairs={{0,12},{12,0},{1,13},{13,1},{2,14},{14,2},{3,15},{15,3},{4,16},{16... | collective-permute-start | bytes 1769480 | tf_op jit(solution)/shard_map/ppermute | solution.py:326
  129.0 12.4 %all-to-all-start.6 = ((f32[12,1,256]{2,1,0:T(1,128)}), f32[12,1,256]{2,1,0:T(1,128)S(1)}, u32[]{:S(2)}, u32[]{:S(2)}) async-start(f32[12,1,256]{2,1,0:T(1,128)} %get-tuple-element.16), calls=%async_computation.6 | async-start | bytes 24576 | tf_op jit(solution)/shard_map/all_to_all | solution.py:44
